TPU v7x, 512 devices: a whole 4x4x16 slice. The times are simulated.
512 devices in a mesh: seq: 16 (over z_lo, y), dp: 32 (over x, z_hi, core).
Axes of the slice: x: 4, y: 4, z: 16 (z_hi: 4, z_lo: 4; z = z_hi * 4 + z_lo), core: 2. Of those that a mesh axis runs over, the one named last changes fastest.
Arguments:
- frames: bfloat16 [32, 3072, 1536], P('dp', 'seq'), may hold values from -6 to 6
- queries: bfloat16 [32, 3072, 1536], P('dp', 'seq'), may hold values from -16 to 16
- keys: bfloat16 [32, 3072, 1536], P('dp', 'seq'), may hold values from -16 to 16
- values: bfloat16 [32, 3072, 1536], P('dp', 'seq'), may hold values from -24 to 24
- lengths: int32 [32], P('dp'), may hold values from 1536 to 3072, as said below
- out_proj: bfloat16 [1536, 1536], P(None, 'dp'), may hold values from -0.15625 to 0.15625
- conv_kernel: float32 [31, 1536], replicated, may hold values from -1 to 1
- cotangent: bfloat16 [32, 3072, 1536], P('dp', 'seq'), may hold values from -6 to 6
Outputs:
- block_out: bfloat16 [32, 3072, 1536], P('dp', 'seq')
- grad_hidden: bfloat16 [32, 3072, 1536], P('dp', 'seq')
- grad_context: bfloat16 [32, 3072, 1536], P('dp', 'seq')
- grad_kernel: float32 [31, 1536], replicated
Inputs may be any that keep to these rules, and one draw needn't show every extreme that they name: `lengths`: one utterance has 3072 valid frames and another 3072 // 2.
All inputs are finite; a program needn't handle non-finite values.
Results may differ from a plain program's by a relative error of at most 0.0062.
Values may be sent and summed in bfloat16 or wider, within the bound.
No kernel may reach another device: no remote copies, remote signals or barrier semaphores. Data moves between devices by JAX's collectives and lax.ppermute only.
A program may use at most 64 MiB of HBM per device.

v0:
```python
import math

import jax
import jax.numpy as jnp
from jax import lax
from jax.sharding import PartitionSpec as P

KERNEL = 31
HEAD_DIM = 96


def with_halo(block, sides, width):
    for axis, dim in sides:
        count = lax.axis_size(axis)
        forward = [(i, i + 1) for i in range(count - 1)]
        backward = [(target, source) for source, target in forward]
        low = lax.ppermute(
            lax.slice_in_dim(block, block.shape[dim] - width, None, axis=dim), axis, forward
        )
        high = lax.ppermute(lax.slice_in_dim(block, 0, width, axis=dim), axis, backward)
        block = jnp.concatenate([low, block, high], axis=dim)
    return block


def attend_heads(query_heads, key_heads, value_heads, key_valid):
    total_frames = query_heads.shape[0]
    head_count = query_heads.shape[1]
    block_rows = math.gcd(total_frames, 1024)
    blocks = query_heads.reshape(total_frames // block_rows, block_rows, head_count, HEAD_DIM)
    softmax_scale = HEAD_DIM ** (-0.5)

    def one_block(query_block):
        scores = (
            jnp.einsum("qhe,khe->hqk", query_block, key_heads, preferred_element_type=jnp.float32)
            * softmax_scale
        )
        scores = jnp.where(key_valid[None, None, :], scores, -jnp.inf)
        largest = jnp.max(scores, axis=-1, keepdims=True)
        expd = jnp.exp(scores - largest)
        weights = (expd / jnp.sum(expd, axis=-1, keepdims=True)).astype(jnp.bfloat16)
        return jnp.einsum(
            "hqk,khe->qhe", weights, value_heads, preferred_element_type=jnp.float32
        ).astype(jnp.bfloat16)

    return lax.map(one_block, blocks).reshape(total_frames, head_count * HEAD_DIM)


def local(frames, queries, keys, values, lengths, out_proj, conv_kernel, cotangent):
    frames_dev = frames.shape[1]
    groups = lax.axis_size("seq")
    length_all = frames_dev * groups
    half_width = KERNEL // 2
    first_frame = lax.axis_index("seq") * frames_dev
    valid_local = first_frame + jnp.arange(frames_dev, dtype=jnp.int32) < lengths[0]
    key_valid = jnp.arange(length_all, dtype=jnp.int32) < lengths[0]
    query_group, key_group, value_group = (
        lax.all_to_all(queries, "seq", split_axis=2, concat_axis=1, tiled=True),
        lax.all_to_all(keys, "seq", split_axis=2, concat_axis=1, tiled=True),
        lax.all_to_all(values, "seq", split_axis=2, concat_axis=1, tiled=True),
    )
    head_count = query_group.shape[2] // HEAD_DIM
    context_heads = attend_heads(
        query_group[0].reshape(length_all, head_count, HEAD_DIM),
        key_group[0].reshape(length_all, head_count, HEAD_DIM),
        value_group[0].reshape(length_all, head_count, HEAD_DIM),
        key_valid,
    )
    context = lax.all_to_all(context_heads[None], "seq", split_axis=1, concat_axis=2, tiled=True)[0]
    mixed = jnp.dot(
        context,
        lax.all_gather(out_proj, "dp", axis=1, tiled=True),
        preferred_element_type=jnp.float32,
    )
    hidden = (frames[0].astype(jnp.float32) + mixed).astype(jnp.bfloat16)
    conv_input = jnp.where(valid_local[:, None], hidden, jnp.zeros((), jnp.bfloat16))
    padded = with_halo(conv_input[None], (("seq", 1),), half_width)[0]
    conv = jnp.zeros((frames_dev, conv_input.shape[1]), jnp.float32)
    for offset in range(KERNEL):
        conv = conv + conv_kernel[offset] * padded[offset : offset + frames_dev].astype(jnp.float32)
    sigma = jax.nn.sigmoid(conv)
    block_out = (hidden.astype(jnp.float32) + conv * sigma).astype(jnp.bfloat16)
    grad_out = cotangent[0].astype(jnp.float32)
    conv_grad = (grad_out * sigma * (1.0 + conv * (1.0 - sigma))).astype(jnp.bfloat16)
    grad_float = conv_grad.astype(jnp.float32)
    kernel_terms = []
    for offset in range(KERNEL):
        kernel_terms.append(
            jnp.sum(grad_float * padded[offset : offset + frames_dev].astype(jnp.float32), axis=0)
        )
    total_count = length_all * lax.axis_size("dp")
    grad_kernel = lax.psum(jnp.stack(kernel_terms), ("seq", "dp")) / math.sqrt(total_count)
    grad_padded = with_halo(conv_grad[None], (("seq", 1),), half_width)[0]
    back = jnp.zeros((frames_dev, conv_input.shape[1]), jnp.float32)
    for offset in range(KERNEL):
        begin = 2 * half_width - offset
        back = back + conv_kernel[offset] * grad_padded[begin : begin + frames_dev].astype(
            jnp.float32
        )
    grad_hidden = (grad_out + jnp.where(valid_local[:, None], back, 0.0)).astype(jnp.bfloat16)
    grad_context = lax.dot_general(
        grad_hidden,
        lax.all_gather(out_proj, "dp", axis=1, tiled=True),
        (((1,), (1,)), ((), ())),
        preferred_element_type=jnp.float32,
    )
    grad_context = grad_context.astype(jnp.bfloat16)
    return (block_out[None], grad_hidden[None], grad_context[None], grad_kernel)


def solution(mesh):
    in_specs = (
        P("dp", "seq", None),
        P("dp", "seq", None),
        P("dp", "seq", None),
        P("dp", "seq", None),
        P("dp"),
        P(None, "dp"),
        P(),
        P("dp", "seq", None),
    )
    out_specs = (P("dp", "seq", None), P("dp", "seq", None), P("dp", "seq", None), P())
    return jax.shard_map(local, mesh=mesh, in_specs=in_specs, out_specs=out_specs, check_vma=False)
```

profile of v0, /device:TPU:1, one launch (start us, length us, event | category | flops | bytes accessed | tf_op | source)
XLA Modules:
  0.0 702.2 jit_solution(153183562824020149)
XLA Ops:
  7.2 3.5 copy.31
  11.2 8.8 %reduce.66 = bf16[1536,192]{1,0:T(8,128)(2,1)S(1)} reduce(bf16[1536,1,192]{2,1,0:T(2,128)(2,1)S(1)} %bitcast.821, bf16[]{:T(256)} %broadcast.335), dimensions={1}, to_apply=%bitcast.766.reduce_sub_computation | reduce | bytes 1179650
  21.8 9.2 %all-to-all-start = ((bf16[16,2,9216]{2,1,0:T(2,128)(2,1)}), bf16[16,2,9216]{2,1,0:T(2,128)(2,1)S(1)}, u32[]{:S(2)}, u32[]{:S(2)}) async-start(bf16[16,2,9216]{2,1,0:T(2,128)(2,1)} %reshape.719), calls=%async_computation | async-start | bytes 1179648 | tf_op jit(solution)/shard_map/all_to_all | solution.py:57
  32.2 8.8 %reduce.67 = bf16[1536,192]{1,0:T(8,128)(2,1)S(1)} reduce(bf16[1536,1,192]{2,1,0:T(2,128)(2,1)S(1)} %bitcast.823, bf16[]{:T(256)} %broadcast.335), dimensions={1}, to_apply=%bitcast.768.reduce_sub_computation | reduce | bytes 1179650
  42.7 2.8 all-to-all-done
  45.5 5.7 all-to-all-start.1
  52.5 8.8 %reduce.68 = bf16[1536,192]{1,0:T(8,128)(2,1)S(1)} reduce(bf16[1536,1,192]{2,1,0:T(2,128)(2,1)S(1)} %bitcast.824, bf16[]{:T(256)} %broadcast.335), dimensions={1}, to_apply=%bitcast.770.reduce_sub_computation | reduce | bytes 1179650
  63.0 2.2 all-to-all-done.1
  65.2 6.1 all-to-all-start.2
  80.2 5.1 all-to-all-done.2
  85.3 4.8 reshape.724
  94.0 28.7 %while.11 = (s32[]{:T(128)}, bf16[3,1024,1,96]{1,3,2,0:T(8,128)(2,1)S(1)}, bf16[3,1024,1,96]{1,3,2,0:T(8,128)(2,1)S(1)}, bf16[3072,1,96]{0,2,1:T(8,128)(2,1)S(1)...) while((s32[]{:T(128)}, bf16[3,1024,1,96]{1,3,2,0:T(8,128)(2,1)S(1)}, ...), condition=%wide.region_3.4_spmd.clone, body=%wide.region_0.3_spmd.clone.sunk | while | flops 1245807616 | bytes 39354456 | solution.py:45
  96.8 2.7 fusion.345
  99.6 4.0 fusion.346
  104.3 2.1 fusion.344
  106.4 2.7 fusion.345
  109.1 4.0 fusion.346
  115.8 2.7 fusion.345
  118.6 4.0 fusion.346
  123.4 17.1 %reduce.69 = bf16[3072,96]{1,0:T(8,128)(2,1)S(1)} reduce(bf16[3072,1,96]{2,1,0:T(2,128)(2,1)S(1)} %bitcast.822, bf16[]{:T(256)} %broadcast.335), dimensions={1}, to_apply=%bitcast.772.reduce_sub_computation | reduce | bytes 1179650
  142.6 6.0 all-to-all-start.3
  149.7 35.3 %all-to-all-done.3 = bf16[16,2,9216]{2,1,0:T(2,128)(2,1)S(1)} async-done(((bf16[16,2,9216]{2,1,0:T(2,128)(2,1)}), bf16[16,2,9216]{2,1,0:T(2,128)(2,1)S(1)}, u32[]{:S(2)}, u32[]{:S(2)}) %all-to-all-start.3) | async-done | bytes 589856 | tf_op jit(solution)/shard_map/all_to_all | solution.py:68
  190.7 4.0 fusion.16
  194.9 2.4 collective-permute-start
  198.7 4.3 collective-permute-done.1
  203.0 6.0 fusion.208
  210.3 4.0 collective-permute-start.3
  214.3 7.4 %fusion.239 = (f32[1536]{0:T(1024)S(1)}, f32[1536]{0:T(1024)S(1)}, f32[1536]{0:T(1024)S(1)}, f32[1536]{0:T(1024)S(1)}, f32[1536]{0:T(1024)S(1)}, /*index=5*/f32[...) fusion(bf16[1,15,1536]{2,1,0:T(8,128)(2,1)S(1)} %collective-permute-done.1, ...), kind=kLoop, calls=%fused_computation.457 | loop fusion | flops 67820544 | bytes 3858624 | tf_op jit(solution)/shard_map/reduce_sum | solution.py:88
  228.5 2.8 stack.127
  231.3 6.6 fusion.209
  237.9 8.9 %fusion.17 = bf16[1,192,1536]{2,1,0:T(8,128)(2,1)} fusion(bf16[1536,1536]{0,1:T(8,128)(2,1)} %all-gather.2.cloned.1.call-done, bf16[1,192,1536]{2,1,0:T(8,128)(2,1)S(1)} %copy-done, bf16[1,192,1536]{2,1,0:T(8,128)(2,1)S(1)} %fusion.208, bf16[1,15,1536]{2,1,0:T(8,128)(2,1)S(1)} %collective-permute-done.3, ...), kind=kOutput, calls=%fused_computation.109 | convolution fusion | flops 961118208 | bytes 6770880 | tf_op jit(solution)/shard_map/dot_general | solution.py:100
  246.8 446.4 %all-reduce.2.cloned.1.call-done = f32[31,1536]{1,0:T(8,128)} async-done(((f32[31,1536]{1,0:T(8,128)}), f32[31,1536]{1,0:T(8,128)}) %all-reduce.2.cloned.1.call-update) | async-done | bytes 190480 | tf_op jit(solution)/shard_map/psum | solution.py:91
  (99 shorter events, 46.6 us)
Async XLA Ops:
  20.0 10.9 %copy-start.1 = (bf16[1,192,1536]{2,1,0:T(8,128)(2,1)S(1)}, bf16[1,192,1536]{2,1,0:T(8,128)(2,1)}, u32[]{:S(2)}) copy-start(bf16[1,192,1536]{2,1,0:T(8,128)(2,1)} %param.12) | copy-start | bytes 1769476
  21.8 23.8 %all-to-all-start = ((bf16[16,2,9216]{2,1,0:T(2,128)(2,1)}), bf16[16,2,9216]{2,1,0:T(2,128)(2,1)S(1)}, u32[]{:S(2)}, u32[]{:S(2)}) async-start(bf16[16,2,9216]{2,1,0:T(2,128)(2,1)} %reshape.719), calls=%async_computation | async-start | bytes 1179648 | tf_op jit(solution)/shard_map/all_to_all | solution.py:57
  42.7 8.5 %copy-start.2 = (bf16[1,192,1536]{2,1,0:T(8,128)(2,1)S(1)}, bf16[1,192,1536]{2,1,0:T(8,128)(2,1)}, u32[]{:S(2)}) copy-start(bf16[1,192,1536]{2,1,0:T(8,128)(2,1)} %param.13) | copy-start | bytes 1769476
  45.5 19.7 %all-to-all-start.1 = ((bf16[16,2,9216]{2,1,0:T(2,128)(2,1)}), bf16[16,2,9216]{2,1,0:T(2,128)(2,1)S(1)}, u32[]{:S(2)}, u32[]{:S(2)}) async-start(bf16[16,2,9216]{2,1,0:T(2,128)(2,1)} %reshape.721), calls=%async_computation.1 | async-start | bytes 1179648 | tf_op jit(solution)/shard_map/all_to_all | solution.py:58
  65.2 20.1 %all-to-all-start.2 = ((bf16[16,2,9216]{2,1,0:T(2,128)(2,1)}), bf16[16,2,9216]{2,1,0:T(2,128)(2,1)}, u32[]{:S(2)}, u32[]{:S(2)}) async-start(bf16[16,2,9216]{2,1,0:T(2,128)(2,1)} %reshape.723), calls=%async_computation.2 | async-start | bytes 1179648 | tf_op jit(solution)/shard_map/all_to_all | solution.py:59
  71.4 119.3 %all-gather.2.cloned.1.call-start = ((), (), s32[]{:S(2)}) async-start(), calls=%async_computation.4 | async-start | bytes 4866048 | tf_op jit(solution)/shard_map/all_gather | solution.py:71
  91.8 2.2 copy-start.3
  140.5 8.8 %copy-start.4 = (f32[31,1536]{1,0:T(8,128)S(1)}, f32[31,1536]{1,0:T(8,128)}, u32[]{:S(2)}) copy-start(f32[31,1536]{1,0:T(8,128)} %param.16) | copy-start | bytes 571396
  142.6 42.4 %all-to-all-start.3 = ((bf16[16,2,9216]{2,1,0:T(2,128)(2,1)}), bf16[16,2,9216]{2,1,0:T(2,128)(2,1)S(1)}, u32[]{:S(2)}, u32[]{:S(2)}) async-start(bf16[16,2,9216]{2,1,0:T(2,128)(2,1)} %reshape.725), calls=%async_computation.3 | async-start | bytes 1179648 | tf_op jit(solution)/shard_map/all_to_all | solution.py:68
  148.6 544.6 %all-reduce.2.cloned.1.call-start = ((), (), s32[]{:S(2)}) async-start(), calls=%async_computation.5 | async-start | bytes 393216 | tf_op jit(solution)/shard_map/psum | solution.py:91
  188.5 2.2 copy-start.5
  194.7 8.3 %copy-start = (bf16[1,192,1536]{2,1,0:T(8,128)(2,1)S(1)}, bf16[1,192,1536]{2,1,0:T(8,128)(2,1)}, u32[]{:S(2)}) copy-start(bf16[1,192,1536]{2,1,0:T(8,128)(2,1)} %param.17) | copy-start | bytes 1769476
  194.9 3.9 collective-permute-start
  197.2 5.8 collective-permute-start.1
  209.0 22.3 %collective-permute-start.2 = (bf16[1,15,1536]{2,1,0:T(8,128)(2,1)S(1)}, bf16[1,15,1536]{2,1,0:T(8,128)(2,1)S(1)}, u32[]{:S(2)}, u32[]{:S(2)}) collective-permute-start(bf16[1,15,1536]{2,1,0:T(8,128)(2,1)S(1)} %get-tuple-element.152), channel_id=1, source_target_pairs={{32,0},{64,32},{96,64},{128,96},{160,128},{192,160},{224,192},{256... | collective-permute-start | bytes 138248 | tf_op jit(solution)/shard_map/ppermute | solution.py:20
  210.3 21.0 %collective-permute-start.3 = (bf16[1,15,1536]{2,1,0:T(8,128)(2,1)S(1)}, bf16[1,15,1536]{2,1,0:T(8,128)(2,1)S(1)}, u32[]{:S(2)}, u32[]{:S(2)}) collective-permute-start(bf16[1,15,1536]{2,1,0:T(8,128)(2,1)S(1)} %get-tuple-element.153), channel_id=1, source_target_pairs={{0,32},{32,64},{64,96},{96,128},{128,160},{160,192},{192,224},{224... | collective-permute-start | bytes 138248 | tf_op jit(solution)/shard_map/ppermute | solution.py:17
Sparse Core Ops, SparseCore 0:
  75.3 107.5 all-gather.1
  231.4 461.7 all-reduce.1
where the time goes:
time: 711 us; the launch traced here: 702 us
  waiting for transfers between devices  496 us (70%)
  other arithmetic  81.8 us (12%)
  local copies, waits for them, and re-layouts  40.2 us (6%)
  starting transfers between devices  36.5 us (5%)
  matrix products  31.2 us (4%)
  between operations  15.9 us (2%)
    psum x1, waiting for transfers between devices, local(): lax.psum(jnp.stack(kernel_terms), ('seq', 'dp')) / math.sqrt(total_count)  446 us
    unnamed x4, other arithmetic  43.7 us
    all_to_all x1, waiting for transfers between devices, local(): lax.all_to_all(context_heads[None], 'seq', split_axis=1, concat_axis=2, t...  35.3 us
    unnamed x25, local copies, waits for them, and re-layouts  22.1 us
  transfers between devices with their start and end apart: 10, of which 6 were waited for; matrix products, arithmetic and copies ran while one was open for 18% of the time, Pallas kernels for 0%

commit v1 on v0

v1 whole, which is shorter than its diff:
```python
import functools
import math

import jax
import jax.numpy as jnp
from jax import lax
from jax.experimental import pallas as pl
from jax.experimental.pallas import tpu as pltpu
from jax.sharding import Mesh
from jax.sharding import PartitionSpec as P

KERNEL = 31
HEAD_DIM = 96
LANES = 128
ROWS = 192
WIDTH = 1536
TILES = WIDTH // LANES
HEADS = 16
LENGTH = ROWS * HEADS
HALF = ROWS // 2
GROUP = 2 * TILES
SLAB = 144
EDGE = 32
QUERY_ROWS = 2 * ROWS
KEY_BLOCK = 512
BF16 = jnp.bfloat16
F32 = jnp.float32
SEQ = ("zl", "y")
DP = ("x", "zh", "c")


def lane_index(rows):
    return lax.broadcasted_iota(jnp.int32, (rows, LANES), 1)


def roll(block, shift):
    return pltpu.roll(block, shift, 1)


def pack_kernel(q_ref, k_ref, v_ref, out_ref):
    lane = lane_index(ROWS)
    low = lane[:SLAB] < HEAD_DIM
    for which, ref in enumerate((q_ref, k_ref, v_ref)):
        tiles = [ref[:, i * LANES : (i + 1) * LANES] for i in range(3)]
        heads = (
            tiles[0],
            roll(jnp.where(lane >= 96, tiles[0], tiles[1]), 32),
            roll(jnp.where(lane >= 64, tiles[1], tiles[2]), 64),
            roll(tiles[2], 96),
        )
        for i, head in enumerate(heads):
            rest = head[SLAB:]
            side = jnp.concatenate([roll(rest, 96), roll(rest, 64), roll(rest, 32)], axis=0)
            out_ref[i, which] = jnp.where(low, head[:SLAB], side)


def pack(queries, keys, values):
    columns = pl.BlockSpec((ROWS, 3 * LANES), lambda i: (0, i))
    return pl.pallas_call(
        pack_kernel,
        grid=(HEADS // 4,),
        in_specs=[columns] * 3,
        out_specs=pl.BlockSpec((4, 3, SLAB, LANES), lambda i: (i, 0, 0, 0)),
        out_shape=jax.ShapeDtypeStruct((HEADS, 3, SLAB, LANES), BF16),
        compiler_params=pltpu.CompilerParams(vmem_limit_bytes=60 * 2**20),
        cost_estimate=pl.CostEstimate(flops=0, bytes_accessed=100_000, transcendentals=0),
        name="pack",
    )(queries, keys, values)


def unpack(block):
    lane = lane_index(48)
    rest = jnp.where(
        lane < 32,
        roll(block[:48], 32),
        jnp.where(lane < 64, roll(block[48:96], 64), roll(block[96:], 96)),
    )
    return jnp.concatenate([block, rest], axis=0)


def attend_kernel(length_ref, qkv_ref, out_ref, kt, vs, qs, os, score_a, score_b):
    scale = math.log2(math.e) * HEAD_DIM ** (-0.5)
    lane = lane_index(ROWS)
    inside = lane < HEAD_DIM
    length = length_ref[0]
    one = jnp.where(lane == HEAD_DIM, 1.0, 0.0).astype(BF16)

    os[:EDGE] = jnp.zeros((EDGE, LANES), BF16)
    os[EDGE + LENGTH :] = jnp.zeros((EDGE, LANES), BF16)

    def prepare(source, carry):
        rows = pl.ds(pl.multiple_of(source * ROWS, 64), ROWS)
        frame = source * ROWS + lax.broadcasted_iota(jnp.int32, (ROWS, LANES), 0)
        hidden_key = jnp.where((lane == HEAD_DIM) & (frame >= length), -1e30, 0.0).astype(BF16)
        qs[rows] = jnp.where(inside, unpack(qkv_ref[source, 0]), one)
        os[pl.ds(pl.multiple_of(EDGE + source * ROWS, 32), ROWS)] = jnp.where(
            inside, unpack(qkv_ref[source, 1]), hidden_key
        )
        vs[rows] = jnp.where(inside, unpack(qkv_ref[source, 2]), one)
        return carry

    lax.fori_loop(0, HEADS, prepare, 0)
    for start in range(0, LENGTH, 256):
        kt[:, start : start + 256] = os[EDGE + start : EDGE + start + 256].T

    def score(block, ref):
        queries = qs[pl.ds(pl.multiple_of(block * QUERY_ROWS, 128), QUERY_ROWS)]
        best = jnp.full((QUERY_ROWS, LANES), -jnp.inf, F32)
        for start in range(0, LENGTH, KEY_BLOCK):
            part = jnp.dot(
                queries, kt[:, start : start + KEY_BLOCK], preferred_element_type=F32
            )
            ref[:, start : start + KEY_BLOCK] = part
            for tile in range(0, KEY_BLOCK, LANES):
                best = jnp.maximum(best, part[:, tile : tile + LANES])
        return jnp.max(best, axis=1, keepdims=True)

    def finish(block, ref, best):
        total = jnp.zeros((QUERY_ROWS, LANES), F32)
        for start in range(0, LENGTH, KEY_BLOCK):
            weights = jnp.exp2((ref[:, start : start + KEY_BLOCK] - best) * scale).astype(BF16)
            total = total + jnp.dot(
                weights, vs[start : start + KEY_BLOCK], preferred_element_type=F32
            )
        context = total / total[:, HEAD_DIM : HEAD_DIM + 1]
        os[pl.ds(pl.multiple_of(EDGE + block * QUERY_ROWS, 32), QUERY_ROWS)] = context.astype(BF16)

    blocks = LENGTH // QUERY_ROWS
    best = score(0, score_a)

    def step(i, best):
        after = score(2 * i + 1, score_b)
        finish(2 * i, score_a, best)
        best = score(2 * i + 2, score_a)
        finish(2 * i + 1, score_b, after)
        return best

    best = lax.fori_loop(0, blocks // 2 - 1, step, best)
    after = score(blocks - 1, score_b)
    finish(blocks - 2, score_a, best)
    finish(blocks - 1, score_b, after)

    halo_lane = lane_index(EDGE)

    def deliver(target, carry):
        begin = target * ROWS
        left = os[pl.ds(pl.multiple_of(begin, 32), EDGE)]
        right = os[pl.ds(pl.multiple_of(begin + EDGE + ROWS, 32), EDGE)]
        own = os[pl.ds(pl.multiple_of(begin + EDGE, 32), ROWS)]
        side = jnp.concatenate(
            [roll(part, shift) for shift in (96, 64, 32) for part in (left, right)], axis=0
        )
        out_ref[target] = jnp.where(inside, own, side)
        return carry

    lax.fori_loop(0, HEADS, deliver, 0)


def attend(length, qkv):
    return pl.pallas_call(
        attend_kernel,
        in_specs=[
            pl.BlockSpec(memory_space=pltpu.SMEM),
            pl.BlockSpec(memory_space=pltpu.VMEM),
        ],
        out_shape=jax.ShapeDtypeStruct((HEADS, ROWS, LANES), BF16),
        scratch_shapes=[
            pltpu.VMEM((LANES, LENGTH), BF16),
            pltpu.VMEM((LENGTH, LANES), BF16),
            pltpu.VMEM((LENGTH, LANES), BF16),
            pltpu.VMEM((LENGTH + 2 * EDGE, LANES), BF16),
            pltpu.VMEM((QUERY_ROWS, LENGTH), F32),
            pltpu.VMEM((QUERY_ROWS, LENGTH), F32),
        ],
        compiler_params=pltpu.CompilerParams(vmem_limit_bytes=48 * 2**20),
        cost_estimate=pl.CostEstimate(flops=0, bytes_accessed=100_000, transcendentals=0),
        name="attend",
    )(length, qkv)


X_STEPS = 160
G_STEPS = 128


def steps(ref, step, column, count=1):
    return ref[pl.ds(pl.multiple_of(step * GROUP + column * 8, 8), 8)]


def to_steps(ref, block, first, count, tile):
    for half in range(2):
        begin = first + half * HALF
        ref[pl.ds(half * TILES + tile, count, stride=GROUP)] = block[begin : begin + count]


def from_steps(ref, half, tile):
    return ref[pl.ds(half * TILES + tile, HALF, stride=GROUP)]


def forward_kernel(
    place_ref, context_ref, project_ref, frames_ref, cot_ref, taps_ref,
    plain_ref, grad_ref, terms_ref, dense, xs, hs, cs, both,
):
    first, length = place_ref[0], place_ref[1]
    rows = ROWS + 2 * EDGE
    lane = lane_index(rows)
    quarter = lane_index(2 * EDGE)
    for group in range(HEADS // 4):
        heads = []
        for i in range(4):
            block = context_ref[4 * group + i]
            halo = jnp.where(
                quarter < 32,
                roll(block[:64], 32),
                jnp.where(quarter < 64, roll(block[64:128], 64), roll(block[128:], 96)),
            )
            heads.append(jnp.concatenate([halo[:EDGE], block, halo[EDGE:]], axis=0))
        second, third, fourth = roll(heads[1], 96), roll(heads[2], 64), roll(heads[3], 32)
        base = 3 * group * LANES
        dense[:, base : base + LANES] = jnp.where(lane < 96, heads[0], second)
        dense[:, base + LANES : base + 2 * LANES] = jnp.where(lane < 64, second, third)
        dense[:, base + 2 * LANES : base + 3 * LANES] = jnp.where(lane < 32, third, fourth)

    frame = first - EDGE + lax.broadcasted_iota(jnp.int32, (rows, LANES), 0)
    valid = (frame >= 0) & (frame < length)
    across = (((1,), (1,)), ((), ()))
    wide = 512
    for start in range(0, WIDTH, wide):
        columns = slice(start, start + wide)
        mixed = lax.dot_general(
            dense[...], project_ref[columns], across, preferred_element_type=F32
        )
        hidden = (frames_ref[:, columns].astype(F32) + mixed).astype(BF16).astype(F32)
        for i in range(wide // LANES):
            tile = start // LANES + i
            block = hidden[:, i * LANES : (i + 1) * LANES]
            to_steps(xs, jnp.where(valid, block, 0.0), 0, X_STEPS, tile)
            to_steps(hs, block, 16, G_STEPS, tile)
            to_steps(
                cs, cot_ref[:, tile * LANES : (tile + 1) * LANES].astype(F32), 0, G_STEPS, tile
            )

    def convolve(index, carry):
        column = index % 3
        step = (index // 3) * 8
        window = [steps(xs, step + 1 + i, column) for i in range(8)]
        sums = [jnp.zeros((8, LANES), F32) for _ in range(8)]
        for k in range(KERNEL):
            tap = taps_ref[pl.ds(pl.multiple_of(k * GROUP + column * 8, 8), 8)]
            sums = [total + tap * value for total, value in zip(sums, window)]
            if k < KERNEL - 1:
                window = window[1:] + [steps(xs, step + k + 9, column)]
        for i, conv in enumerate(sums):
            at = pl.ds(pl.multiple_of((step + i) * GROUP + column * 8, 8), 8)
            sigma = jax.nn.sigmoid(conv)
            plain_ref[at] = hs[at] + conv * sigma
            grad = cs[at] * sigma * (1.0 + conv * (1.0 - sigma))
            grad_ref[at] = grad.astype(BF16).astype(F32)
        return carry

    lax.fori_loop(0, 3 * G_STEPS // 8, convolve, 0)

    for column in range(3):

        def gather(block, sums):
            step = block * 8
            grads = [steps(grad_ref, step + 16 + i, column) for i in range(8)]
            sums = list(sums)
            for offset in range(KERNEL + 7):
                value = steps(xs, step + 17 + offset, column)
                for i in range(8):
                    if 0 <= offset - i < KERNEL:
                        sums[offset - i] = sums[offset - i] + grads[i] * value
            return tuple(sums)

        zero = tuple(jnp.zeros((8, LANES), F32) for _ in range(KERNEL))
        sums = lax.fori_loop(0, HALF // 8, gather, zero)
        for k in range(KERNEL):
            both[k, column * 8 : column * 8 + 8] = sums[k]
    terms_ref[...] = jnp.zeros((KERNEL + 1, 16, LANES), F32)
    terms_ref[:KERNEL, :TILES] = both[:, :TILES] + both[:, TILES:]


def forward(place, context, project, frames, cotangent, taps):
    return pl.pallas_call(
        forward_kernel,
        in_specs=[pl.BlockSpec(memory_space=pltpu.SMEM)]
        + [pl.BlockSpec(memory_space=pltpu.VMEM)] * 5,
        out_shape=[
            jax.ShapeDtypeStruct((G_STEPS * GROUP, LANES), F32),
            jax.ShapeDtypeStruct((G_STEPS * GROUP, LANES), F32),
            jax.ShapeDtypeStruct((KERNEL + 1, 16, LANES), F32),
        ],
        scratch_shapes=[
            pltpu.VMEM((ROWS + 2 * EDGE, WIDTH), BF16),
            pltpu.VMEM((X_STEPS * GROUP, LANES), F32),
            pltpu.VMEM((G_STEPS * GROUP, LANES), F32),
            pltpu.VMEM((G_STEPS * GROUP, LANES), F32),
            pltpu.VMEM((KERNEL, GROUP, LANES), F32),
        ],
        compiler_params=pltpu.CompilerParams(vmem_limit_bytes=48 * 2**20),
        cost_estimate=pl.CostEstimate(
            flops=2 * 256 * WIDTH * WIDTH, bytes_accessed=10_000_000, transcendentals=400_000
        ),
        name="forward",
    )(place, context, project, frames, cotangent, taps)


def backward_kernel(
    place_ref, plain_ref, grad_ref, cot_ref, taps_ref, project_ref,
    block_ref, hidden_ref, context_ref, bs,
):
    first, length = place_ref[0], place_ref[1]

    def convolve(index, carry):
        column = index % 3
        step = (index // 3) * 8
        window = [steps(grad_ref, step + 1 + i, column) for i in range(8)]
        sums = [jnp.zeros((8, LANES), F32) for _ in range(8)]
        for k in range(KERNEL):
            tap = taps_ref[pl.ds(pl.multiple_of((KERNEL - 1 - k) * GROUP + column * 8, 8), 8)]
            sums = [total + tap * value for total, value in zip(sums, window)]
            if k < KERNEL - 1:
                window = window[1:] + [steps(grad_ref, step + k + 9, column)]
        for i, total in enumerate(sums):
            bs[pl.ds(pl.multiple_of((step + i) * GROUP + column * 8, 8), 8)] = total
        return carry

    lax.fori_loop(0, 3 * HALF // 8, convolve, 0)
    frame = first + lax.broadcasted_iota(jnp.int32, (HALF, LANES), 0)
    for half in range(2):
        rows = slice(half * HALF, (half + 1) * HALF)
        valid = frame + half * HALF < length
        for tile in range(TILES):
            columns = slice(tile * LANES, (tile + 1) * LANES)
            plain = plain_ref[pl.ds(16 * GROUP + half * TILES + tile, HALF, stride=GROUP)]
            block_ref[rows, columns] = plain.astype(BF16)
            back = jnp.where(valid, from_steps(bs, half, tile), 0.0)
            cot = cot_ref[16 + half * HALF : 16 + (half + 1) * HALF, columns].astype(F32)
            hidden_ref[rows, columns] = (cot + back).astype(BF16)
    wide = 256
    for start in range(0, WIDTH, wide):
        columns = slice(start, start + wide)
        part = jnp.dot(hidden_ref[...], project_ref[:, columns], preferred_element_type=F32)
        context_ref[:, columns] = part.astype(BF16)


def backward(place, plain, grad, cotangent, taps, project):
    return pl.pallas_call(
        backward_kernel,
        in_specs=[pl.BlockSpec(memory_space=pltpu.SMEM)]
        + [pl.BlockSpec(memory_space=pltpu.VMEM)] * 5,
        out_shape=[jax.ShapeDtypeStruct((ROWS, WIDTH), BF16)] * 3,
        scratch_shapes=[pltpu.VMEM((HALF * GROUP, LANES), F32)],
        compiler_params=pltpu.CompilerParams(vmem_limit_bytes=48 * 2**20),
        cost_estimate=pl.CostEstimate(
            flops=2 * ROWS * WIDTH * WIDTH, bytes_accessed=12_000_000, transcendentals=0
        ),
        name="backward",
    )(place, plain, grad, cotangent, taps, project)


def spread(array, axes):
    copies = jnp.broadcast_to(array[None], (lax.axis_size(axes), *array.shape))
    return lax.all_to_all(copies, axes, 0, 0, tiled=True)


def local(frames, queries, keys, values, lengths, out_proj, conv_kernel, cotangent):
    seq = lax.axis_index(SEQ)
    place = jnp.stack([seq * ROWS, lengths[0]]).astype(jnp.int32)

    project = lax.all_gather(out_proj.T, DP, axis=0, tiled=True)
    qkv = lax.all_to_all(pack(queries[0], keys[0], values[0]), SEQ, 0, 0, tiled=True)

    qkv, frames, cotangent = lax.optimization_barrier((qkv, frames, cotangent))
    edge = jnp.concatenate([frames[0, -EDGE:], cotangent[0, -16:]], axis=0)
    forward_pairs = [(i, i + 1) for i in range(HEADS - 1)]
    low = lax.ppermute(edge, SEQ, forward_pairs)
    edge = jnp.concatenate([frames[0, :EDGE], cotangent[0, :16]], axis=0)
    high = lax.ppermute(edge, SEQ, [(target, source) for source, target in forward_pairs])
    wide_frames = jnp.concatenate([low[:EDGE], frames[0], high[:EDGE]], axis=0)
    wide_cot = jnp.concatenate([low[EDGE:], cotangent[0], high[EDGE:]], axis=0)
    taps = conv_kernel.reshape(KERNEL, 1, TILES, LANES)
    taps = jnp.concatenate([taps, taps], axis=1).reshape(KERNEL * GROUP, LANES)

    heads, wide_frames, wide_cot, taps = lax.optimization_barrier(
        (attend(lengths, qkv), wide_frames, wide_cot, taps)
    )
    context = lax.all_to_all(heads, SEQ, 0, 0, tiled=True)
    plain, grad, terms = forward(place, context, project, wide_frames, wide_cot, taps)

    near_axes = ("zl", "y", "c")
    part = jnp.sum(lax.all_to_all(terms, near_axes, 0, 0, tiled=True), axis=0)
    part = jnp.sum(spread(part, ("x", "zh")), axis=0)
    block, hidden, grad_context = backward(place, plain, grad, wide_cot, taps, project)
    part, block = lax.optimization_barrier((part, block))
    whole = spread(part, near_axes)[:KERNEL, :TILES].reshape(KERNEL, WIDTH)
    grad_kernel = whole / math.sqrt(LENGTH * 32)

    return (block[None], hidden[None], grad_context[None], grad_kernel)


def solution(mesh):
    fine = Mesh(mesh.devices.reshape(4, 4, 4, 4, 2), ("zl", "y", "x", "zh", "c"))
    block = P(DP, SEQ, None)
    in_specs = (block, block, block, block, P(DP), P(None, DP), P(), block)
    out_specs = (block, block, block, P())
    return jax.shard_map(local, mesh=fine, in_specs=in_specs, out_specs=out_specs, check_vma=False)
```

time: 711 us -> 234 us (0.33); the launches traced: 702 us -> 233 us
  waiting for transfers between devices: 496 us -> 88 us
  other arithmetic: 81.8 us -> 1.63 us
  Pallas kernels: 0 us -> 42.4 us
  blocking collectives: 0 us -> 36.4 us
  local copies, waits for them, and re-layouts: 40.2 us -> 7.61 us
  matrix products: 31.2 us -> 0 us
    psum x1 -> x0, waiting for transfers between devices: 446 us -> none  [local(): lax.psum(jnp.stack(kernel_terms), ('seq', 'dp')) / math.sqrt(total_count)]
    unnamed x4 -> x0, other arithmetic: 43.7 us -> none
    pallas_call x0 -> x4, Pallas kernels: none -> 42.4 us  [the longest x1 16.7 us: attend(): pl.pallas_call(attend_kernel, in_specs=[pl.BlockSpec(memory_space=pltpu.S...]
    all_gather x1, waiting for transfers between devices: 0.02 us -> 36.7 us  [local(): project = lax.all_gather(out_proj.T, DP, axis=0, tiled=True)]
    all_to_all x0 -> x2, blocking collectives: none -> 36.4 us  [the longest x1 19.3 us: local(): part = jnp.sum(lax.all_to_all(terms, near_axes, 0, 0, tiled=True), axis=0)]
    dot_general x8 -> x0, matrix products: 31.2 us -> none  [the longest x3 12.1 us: one_block(): jnp.einsum('hqk,khe->qhe', weights, value_heads, preferred_element_type=j...]
    reduce_sum x9 -> x2, other arithmetic: 21.9 us -> 0.05 us  [the longest x1 0.04 us: local(): part = jnp.sum(lax.all_to_all(terms, near_axes, 0, 0, tiled=True), axis=0)]
    unnamed x25 -> x16, local copies, waits for them, and re-layouts: 22.1 us -> 5.92 us
  transfers between devices with their start and end apart: 10 -> 6, of which waited for: 6 -> 4; matrix products, arithmetic and copies ran while one was open for 18% -> 1% of each run, Pallas kernels for 0% -> 11%
where the time goes in v1:
time: 234 us; the launch traced here: 233 us
  waiting for transfers between devices  88 us (38%)
  Pallas kernels  42.4 us (18%)
  starting transfers between devices  42 us (18%)
  blocking collectives  36.4 us (16%)
  between operations  14.9 us (6%)
  local copies, waits for them, and re-layouts  7.61 us (3%)
    all_to_all x1, waiting for transfers between devices, local(): lax.all_to_all(pack(queries[0], keys[0], values[0]), SEQ, 0, 0, tiled=True)  39 us
    all_gather x1, waiting for transfers between devices, local(): project = lax.all_gather(out_proj.T, DP, axis=0, tiled=True)  36.7 us
    all_to_all x1, blocking collectives, local(): part = jnp.sum(lax.all_to_all(terms, near_axes, 0, 0, tiled=True), axis=0)  19.3 us
    all_to_all x1, blocking collectives, spread(): return lax.all_to_all(copies, axes, 0, 0, tiled=True)  17.1 us
    pallas_call x1, Pallas kernels, attend(): pl.pallas_call(attend_kernel, in_specs=[pl.BlockSpec(memory_space=pltpu.S...  16.7 us
    all_to_all x1, starting transfers between devices, local(): context = lax.all_to_all(heads, SEQ, 0, 0, tiled=True)  16.1 us
    pallas_call x1, Pallas kernels, forward(): pl.pallas_call(forward_kernel, in_specs=[pl.BlockSpec(memory_space=pltpu....  12.9 us
    all_to_all x1, starting transfers between devices, spread(): return lax.all_to_all(copies, axes, 0, 0, tiled=True)  11.3 us
  transfers between devices with their start and end apart: 6, of which 4 were waited for; matrix products, arithmetic and copies ran while one was open for 1% of the time, Pallas kernels for 11%

profile of v1, /device:TPU:1, one launch (start us, length us, event | category | flops | bytes accessed | tf_op | source)
XLA Modules:
  0.0 232.9 jit_solution(17509310920037513343)
XLA Ops:
  7.2 4.5 %pack.1 = bf16[16,3,144,128]{3,2,1,0:T(8,128)(2,1)} custom-call(bf16[192,1536]{1,0:T(8,128)(2,1)} %bitcast.24, bf16[192,1536]{1,0:T(8,128)(2,1)} %bitcast.25, bf16[192,1536]{1,0:T(8,128)(2,1)} %bitcast.26), custom_call_target="tpu_custom_call" | custom-call | bytes 100000 | tf_op jit(solution)/shard_map/pack/pallas_call | solution.py:59
  11.7 9.3 %all-to-all-start = ((bf16[16,3,144,128]{3,2,1,0:T(8,128)(2,1)}), bf16[16,3,144,128]{3,2,1,0:T(8,128)(2,1)S(1)}, u32[]{:S(2)}, u32[]{:S(2)}) async-start(bf16[16,3,144,128]{3,2,1,0:T(8,128)(2,1)} %pack.1), calls=%async_computation | async-start | bytes 3538944 | tf_op jit(solution)/shard_map/all_to_all | solution.py:372
  21.0 0.0 all-gather.2.cloned.1.call-start
  21.1 0.7 all-gather.2.cloned.1.call-update
  21.7 39.0 %all-to-all-done.qkv_ref = bf16[16,3,144,128]{3,2,1,0:T(8,128)(2,1)S(1)} async-done(((bf16[16,3,144,128]{3,2,1,0:T(8,128)(2,1)}), bf16[16,3,144,128]{3,2,1,0:T(8,128)(2,1)S(1)}, u32[]{:S(2)}, u32[]{:S(2)}) %all-to-all-start) | async-done | bytes 1769504 | tf_op jit(solution)/shard_map/all_to_all | solution.py:372
  60.8 0.8 slice_bitcast_fusion.3
  61.6 0.7 pad_maximum_fusion.4
  62.3 1.3 collective-permute-start.1
  63.6 0.7 pad_maximum_fusion.3
  64.2 4.0 %collective-permute-start = (bf16[48,1536]{1,0:T(8,128)(2,1)}, bf16[48,1536]{1,0:T(8,128)(2,1)S(1)}, u32[]{:S(2)}, u32[]{:S(2)}) collective-permute-start(bf16[48,1536]{1,0:T(8,128)(2,1)} %pad_maximum_fusion.3), channel_id=1, source_target_pairs={{0,32},{32,64},{64,96},{96,128},{128,160},{160,192},{192,224},{224... | collective-permute-start | bytes 442376 | tf_op jit(solution)/shard_map/ppermute | solution.py:377
  69.0 0.1 copy.15
  69.1 0.0 copy-start.5
  69.1 16.7 %attend.1 = bf16[16,192,128]{2,1,0:T(8,128)(2,1)} custom-call(s32[1]{0:T(128)S(6)} %copy.17.length_ref, bf16[16,3,144,128]{3,2,1,0:T(8,128)(2,1)S(1)} %all-to-all-done.qkv_ref), custom_call_target="tpu_custom_call" | custom-call | bytes 100000 | tf_op jit(solution)/shard_map/attend/pallas_call | solution.py:160
  85.9 0.0 collective-permute-done.1
  85.9 0.0 collective-permute-done
  86.0 0.1 pad_maximum_fusion.frames_ref
  86.0 16.1 %all-to-all-start.1 = ((bf16[16,192,128]{2,1,0:T(8,128)(2,1)}), bf16[16,192,128]{2,1,0:T(8,128)(2,1)S(1)}, u32[]{:S(2)}, u32[]{:S(2)}) async-start(bf16[16,192,128]{2,1,0:T(8,128)(2,1)} %attend.1), calls=%async_computation.1 | async-start | bytes 1572864 | tf_op jit(solution)/shard_map/all_to_all | solution.py:388
  102.2 0.1 pad_add_fusion.place_ref
  102.3 36.7 %all-gather.2.cloned.1.call-done.project_ref = bf16[1536,1536]{1,0:T(8,128)(2,1)} async-done(((bf16[48,1536]{1,0:T(8,128)(2,1)}), bf16[1536,1536]{1,0:T(8,128)(2,1)}) %all-gather.2.cloned.1.call-update) | async-done | bytes 4718608 | tf_op jit(solution)/shard_map/all_gather | solution.py:371
  138.9 6.8 %all-to-all-done.1.context_ref = bf16[16,192,128]{2,1,0:T(8,128)(2,1)S(1)} async-done(((bf16[16,192,128]{2,1,0:T(8,128)(2,1)}), bf16[16,192,128]{2,1,0:T(8,128)(2,1)S(1)}, u32[]{:S(2)}, u32[]{:S(2)}) %all-to-all-start.1) | async-done | bytes 786464 | tf_op jit(solution)/shard_map/all_to_all | solution.py:388
  145.7 12.9 %forward.1 = (f32[3072,128]{1,0:T(8,128)S(1)}, f32[3072,128]{1,0:T(8,128)S(1)}, f32[32,16,128]{2,1,0:T(8,128)S(1)}) custom-call(s32[2]{0:T(128)S(1)} %pad_add_fusion.place_ref, bf16[16,192,128]{2,1,0:T(8,128)(2,1)S(1)} %all-to-all-done.1.context_ref, bf16[1536,1536]{1,0:T(8,128)(2,1)} %all-gather.2.cloned.1.call-done.project_ref, ...), custom_call_target="tpu_custom_call" | custom-call | flops 1207959552 | bytes 10000000 | tf_op jit(solution)/shard_map/forward/pallas_call | solution.py:284
  158.6 1.2 copy-done
  159.8 1.1 copy-done.2
  161.0 19.3 %all_to_all.25 = f32[32,16,128]{2,1,0:T(8,128)S(1)} all-to-all(f32[32,16,128]{2,1,0:T(8,128)S(1)} %get-tuple-element.26), channel_id=1, replica_groups=mesh['zl'=4,'y'=4,'x'=4,'zh'=4,'c'=2] {'zl','y','c'}, dimensions={0} | all-to-all | bytes 524288 | tf_op jit(solution)/shard_map/all_to_all | solution.py:392
  180.3 0.7 broadcast_in_dim.10
  181.0 11.3 %all-to-all-start.3 = ((f32[16,16,128]{2,1,0:T(8,128)}), f32[16,16,128]{2,1,0:T(8,128)S(1)}, u32[]{:S(2)}, u32[]{:S(2)}) async-start(f32[16,16,128]{2,1,0:T(8,128)} %broadcast_in_dim.10), calls=%async_computation.3 | async-start | bytes 262144 | tf_op jit(solution)/shard_map/all_to_all | solution.py:364
  192.3 1.4 copy-done.1
  193.7 1.4 copy-done.3
  195.1 8.2 %backward.1 = (bf16[192,1536]{1,0:T(8,128)(2,1)}, bf16[192,1536]{1,0:T(8,128)(2,1)}, bf16[192,1536]{1,0:T(8,128)(2,1)}) custom-call(s32[2]{0:T(128)S(1)} %pad_add_fusion.place_ref, f32[3072,128]{1,0:T(8,128)S(1)} %copy-done.1, f32[3072,128]{1,0:T(8,128)S(1)} %copy-done.3, bf16[224,1536]{1,0:T(8,128)(2,1)S(1)} %pad_maximum_fusion.1.cot_ref, ...), custom_call_target="tpu_custom_call" | custom-call | flops 905969664 | bytes 12000000 | tf_op jit(solution)/shard_map/backward/pallas_call | solution.py:348
  203.3 4.8 %all-to-all-done.3 = f32[16,16,128]{2,1,0:T(8,128)S(1)} async-done(((f32[16,16,128]{2,1,0:T(8,128)}), f32[16,16,128]{2,1,0:T(8,128)S(1)}, u32[]{:S(2)}, u32[]{:S(2)}) %all-to-all-start.3) | async-done | bytes 131104 | tf_op jit(solution)/shard_map/all_to_all | solution.py:364
  208.2 17.1 %all_to_all.26 = f32[32,16,128]{2,1,0:T(8,128)S(1)} all-to-all(f32[32,16,128]{2,1,0:T(8,128)S(1)} %broadcast_in_dim.25), channel_id=1, replica_groups=mesh['zl'=4,'y'=4,'x'=4,'zh'=4,'c'=2] {'zl','y','c'}, dimensions={0} | all-to-all | bytes 524288 | tf_op jit(solution)/shard_map/all_to_all | solution.py:364
  225.3 0.7 copy.16
  (23 shorter events, 0.3 us)
Async XLA Ops:
  11.7 49.9 %copy-start.4 = (bf16[1,192,1536]{2,1,0:T(8,128)(2,1)S(1)}, bf16[1,192,1536]{2,1,0:T(8,128)(2,1)}, u32[]{:S(2)}) copy-start(bf16[1,192,1536]{2,1,0:T(8,128)(2,1)} %param.8) | copy-start | bytes 1769476
  11.7 57.2 %copy-start.6 = (f32[31,1536]{1,0:T(8,128)S(1)}, f32[31,1536]{1,0:T(8,128)}, u32[]{:S(2)}) copy-start(f32[31,1536]{1,0:T(8,128)} %param.14) | copy-start | bytes 571396
  11.7 49.1 %all-to-all-start = ((bf16[16,3,144,128]{3,2,1,0:T(8,128)(2,1)}), bf16[16,3,144,128]{3,2,1,0:T(8,128)(2,1)S(1)}, u32[]{:S(2)}, u32[]{:S(2)}) async-start(bf16[16,3,144,128]{3,2,1,0:T(8,128)(2,1)} %pack.1), calls=%async_computation | async-start | bytes 3538944 | tf_op jit(solution)/shard_map/all_to_all | solution.py:372
  21.0 117.9 %all-gather.2.cloned.1.call-start = ((), (), s32[]{:S(2)}) async-start(), calls=%async_computation.5 | async-start | bytes 4866048 | tf_op jit(solution)/shard_map/all_gather | solution.py:371
  62.3 23.6 %collective-permute-start.1 = (bf16[48,1536]{1,0:T(8,128)(2,1)}, bf16[48,1536]{1,0:T(8,128)(2,1)S(1)}, u32[]{:S(2)}, u32[]{:S(2)}) collective-permute-start(bf16[48,1536]{1,0:T(8,128)(2,1)} %pad_maximum_fusion.4), channel_id=1, source_target_pairs={{32,0},{64,32},{96,64},{128,96},{160,128},{192,160},{224,192},{256... | collective-permute-start | bytes 442376 | tf_op jit(solution)/shard_map/ppermute | solution.py:379
  64.2 21.6 %collective-permute-start = (bf16[48,1536]{1,0:T(8,128)(2,1)}, bf16[48,1536]{1,0:T(8,128)(2,1)S(1)}, u32[]{:S(2)}, u32[]{:S(2)}) collective-permute-start(bf16[48,1536]{1,0:T(8,128)(2,1)} %pad_maximum_fusion.3), channel_id=1, source_target_pairs={{0,32},{32,64},{64,96},{96,128},{128,160},{160,192},{192,224},{224... | collective-permute-start | bytes 442376 | tf_op jit(solution)/shard_map/ppermute | solution.py:377
  69.1 16.8 %copy-start.5 = (bf16[1,192,1536]{2,1,0:T(8,128)(2,1)S(1)}, bf16[1,192,1536]{2,1,0:T(8,128)(2,1)}, u32[]{:S(2)}) copy-start(bf16[1,192,1536]{2,1,0:T(8,128)(2,1)} %param.15) | copy-start | bytes 1769476
  86.0 59.7 %all-to-all-start.1 = ((bf16[16,192,128]{2,1,0:T(8,128)(2,1)}), bf16[16,192,128]{2,1,0:T(8,128)(2,1)S(1)}, u32[]{:S(2)}, u32[]{:S(2)}) async-start(bf16[16,192,128]{2,1,0:T(8,128)(2,1)} %attend.1), calls=%async_computation.1 | async-start | bytes 1572864 | tf_op jit(solution)/shard_map/all_to_all | solution.py:388
  158.6 1.2 copy-start
  159.8 1.1 copy-start.2
  181.0 27.1 %all-to-all-start.3 = ((f32[16,16,128]{2,1,0:T(8,128)}), f32[16,16,128]{2,1,0:T(8,128)S(1)}, u32[]{:S(2)}, u32[]{:S(2)}) async-start(f32[16,16,128]{2,1,0:T(8,128)} %broadcast_in_dim.10), calls=%async_computation.3 | async-start | bytes 262144 | tf_op jit(solution)/shard_map/all_to_all | solution.py:364
  192.3 1.4 copy-start.1
  193.7 1.4 copy-start.3
Sparse Core Ops, SparseCore 0:
  25.0 113.9 all-gather.1

commit v2 on v1

--- a/solution.py
+++ b/solution.py
@@ -63,7 +63,7 @@
         out_specs=pl.BlockSpec((4, 3, SLAB, LANES), lambda i: (i, 0, 0, 0)),
         out_shape=jax.ShapeDtypeStruct((HEADS, 3, SLAB, LANES), BF16),
         compiler_params=pltpu.CompilerParams(vmem_limit_bytes=60 * 2**20),
-        cost_estimate=pl.CostEstimate(flops=0, bytes_accessed=100_000, transcendentals=0),
+        cost_estimate=pl.CostEstimate(flops=0, bytes_accessed=4_000_000, transcendentals=0),
         name="pack",
     )(queries, keys, values)
 
@@ -173,10 +173,16 @@
             pltpu.VMEM((QUERY_ROWS, LENGTH), F32),
         ],
         compiler_params=pltpu.CompilerParams(vmem_limit_bytes=48 * 2**20),
-        cost_estimate=pl.CostEstimate(flops=0, bytes_accessed=100_000, transcendentals=0),
+        cost_estimate=pl.CostEstimate(
+            flops=4 * LENGTH * LENGTH * 128,
+            bytes_accessed=3_000_000,
+            transcendentals=LENGTH * LENGTH,
+        ),
         name="attend",
     )(length, qkv)
 
+
+BLOCK = WIDTH // 4
 
 X_STEPS = 160
 G_STEPS = 128
@@ -192,15 +198,21 @@
         ref[pl.ds(half * TILES + tile, count, stride=GROUP)] = block[begin : begin + count]
 
 
+def project_blocks(x, refs):
+    blocks = []
+    for shift, (near, far) in enumerate(zip(refs[:4], refs[4:])):
+        start = pl.multiple_of(lax.rem(x + 4 - shift, 4) * BLOCK, LANES)
+        blocks.append((start, BLOCK, near, far))
+    return blocks
+
+
 def from_steps(ref, half, tile):
     return ref[pl.ds(half * TILES + tile, HALF, stride=GROUP)]
 
 
-def forward_kernel(
-    place_ref, context_ref, project_ref, frames_ref, cot_ref, taps_ref,
-    plain_ref, grad_ref, terms_ref, dense, xs, hs, cs, both,
-):
-    first, length = place_ref[0], place_ref[1]
+def forward_kernel(place_ref, context_ref, frames_ref, cot_ref, taps_ref, *refs):
+    project_refs, (plain_ref, grad_ref, terms_ref, dense, xs, hs, cs, both) = refs[:8], refs[8:]
+    x, core, first, length = place_ref[0], place_ref[1], place_ref[2], place_ref[3]
     rows = ROWS + 2 * EDGE
     lane = lane_index(rows)
     quarter = lane_index(2 * EDGE)
@@ -222,22 +234,23 @@
 
     frame = first - EDGE + lax.broadcasted_iota(jnp.int32, (rows, LANES), 0)
     valid = (frame >= 0) & (frame < length)
+    for tile in range(TILES):
+        block = cot_ref[:, tile * LANES : (tile + 1) * LANES].astype(F32)
+        to_steps(cs, block, 0, G_STEPS, tile)
     across = (((1,), (1,)), ((), ()))
-    wide = 512
-    for start in range(0, WIDTH, wide):
-        columns = slice(start, start + wide)
-        mixed = lax.dot_general(
-            dense[...], project_ref[columns], across, preferred_element_type=F32
-        )
-        hidden = (frames_ref[:, columns].astype(F32) + mixed).astype(BF16).astype(F32)
+    half_width = WIDTH // 2
+    near = dense[:, pl.ds(pl.multiple_of(core * half_width, LANES), half_width)]
+    far = dense[:, pl.ds(pl.multiple_of((1 - core) * half_width, LANES), half_width)]
+    for start, wide, near_ref, far_ref in project_blocks(x, project_refs):
+        mixed = lax.dot_general(near, near_ref[...], across, preferred_element_type=F32)
+        mixed += lax.dot_general(far, far_ref[...], across, preferred_element_type=F32)
+        columns = frames_ref[:, pl.ds(start, wide)]
+        hidden = (columns.astype(F32) + mixed).astype(BF16).astype(F32)
         for i in range(wide // LANES):
             tile = start // LANES + i
             block = hidden[:, i * LANES : (i + 1) * LANES]
             to_steps(xs, jnp.where(valid, block, 0.0), 0, X_STEPS, tile)
             to_steps(hs, block, 16, G_STEPS, tile)
-            to_steps(
-                cs, cot_ref[:, tile * LANES : (tile + 1) * LANES].astype(F32), 0, G_STEPS, tile
-            )
 
     def convolve(index, carry):
         column = index % 3
@@ -280,11 +293,11 @@
     terms_ref[:KERNEL, :TILES] = both[:, :TILES] + both[:, TILES:]
 
 
-def forward(place, context, project, frames, cotangent, taps):
+def forward(place, context, frames, cotangent, taps, project):
     return pl.pallas_call(
         forward_kernel,
         in_specs=[pl.BlockSpec(memory_space=pltpu.SMEM)]
-        + [pl.BlockSpec(memory_space=pltpu.VMEM)] * 5,
+        + [pl.BlockSpec(memory_space=pltpu.VMEM)] * 12,
         out_shape=[
             jax.ShapeDtypeStruct((G_STEPS * GROUP, LANES), F32),
             jax.ShapeDtypeStruct((G_STEPS * GROUP, LANES), F32),
@@ -302,14 +315,12 @@
             flops=2 * 256 * WIDTH * WIDTH, bytes_accessed=10_000_000, transcendentals=400_000
         ),
         name="forward",
-    )(place, context, project, frames, cotangent, taps)
-
-
-def backward_kernel(
-    place_ref, plain_ref, grad_ref, cot_ref, taps_ref, project_ref,
-    block_ref, hidden_ref, context_ref, bs,
-):
-    first, length = place_ref[0], place_ref[1]
+    )(place, context, frames, cotangent, taps, *project)
+
+
+def backward_kernel(place_ref, plain_ref, grad_ref, cot_ref, taps_ref, *refs):
+    project_refs, (block_ref, hidden_ref, context_ref, bs) = refs[:8], refs[8:]
+    x, core, first, length = place_ref[0], place_ref[1], place_ref[2], place_ref[3]
 
     def convolve(index, carry):
         column = index % 3
@@ -337,18 +348,27 @@
             back = jnp.where(valid, from_steps(bs, half, tile), 0.0)
             cot = cot_ref[16 + half * HALF : 16 + (half + 1) * HALF, columns].astype(F32)
             hidden_ref[rows, columns] = (cot + back).astype(BF16)
-    wide = 256
-    for start in range(0, WIDTH, wide):
-        columns = slice(start, start + wide)
-        part = jnp.dot(hidden_ref[...], project_ref[:, columns], preferred_element_type=F32)
-        context_ref[:, columns] = part.astype(BF16)
+    half_width = WIDTH // 2
+    blocks = [
+        (hidden_ref[:, pl.ds(start, wide)], near_ref, far_ref)
+        for start, wide, near_ref, far_ref in project_blocks(x, project_refs)
+    ]
+    step = 256
+    for which, begin in ((1, core * half_width), (2, (1 - core) * half_width)):
+        for start in range(0, half_width, step):
+            total = jnp.zeros((ROWS, step), F32)
+            for block in blocks:
+                part = block[which][:, start : start + step]
+                total = total + jnp.dot(block[0], part, preferred_element_type=F32)
+            columns = pl.ds(pl.multiple_of(begin + start, LANES), step)
+            context_ref[:, columns] = total.astype(BF16)
 
 
 def backward(place, plain, grad, cotangent, taps, project):
     return pl.pallas_call(
         backward_kernel,
         in_specs=[pl.BlockSpec(memory_space=pltpu.SMEM)]
-        + [pl.BlockSpec(memory_space=pltpu.VMEM)] * 5,
+        + [pl.BlockSpec(memory_space=pltpu.VMEM)] * 12,
         out_shape=[jax.ShapeDtypeStruct((ROWS, WIDTH), BF16)] * 3,
         scratch_shapes=[pltpu.VMEM((HALF * GROUP, LANES), F32)],
         compiler_params=pltpu.CompilerParams(vmem_limit_bytes=48 * 2**20),
@@ -356,7 +376,7 @@
             flops=2 * ROWS * WIDTH * WIDTH, bytes_accessed=12_000_000, transcendentals=0
         ),
         name="backward",
-    )(place, plain, grad, cotangent, taps, project)
+    )(place, plain, grad, cotangent, taps, *project)
 
 
 def spread(array, axes):
@@ -366,12 +386,28 @@
 
 def local(frames, queries, keys, values, lengths, out_proj, conv_kernel, cotangent):
     seq = lax.axis_index(SEQ)
-    place = jnp.stack([seq * ROWS, lengths[0]]).astype(jnp.int32)
-
-    project = lax.all_gather(out_proj.T, DP, axis=0, tiled=True)
-    qkv = lax.all_to_all(pack(queries[0], keys[0], values[0]), SEQ, 0, 0, tiled=True)
-
-    qkv, frames, cotangent = lax.optimization_barrier((qkv, frames, cotangent))
+    core = lax.axis_index("c")
+    place = jnp.stack([lax.axis_index("x"), core, seq * ROWS, lengths[0]]).astype(jnp.int32)
+
+    rows = lax.all_gather(out_proj.T, "c", axis=0, tiled=True)
+    quarter = rows.shape[0] // 4
+    share = lax.dynamic_slice(
+        rows, (lax.axis_index("y") * quarter, core * (WIDTH // 2)), (quarter, WIDTH // 2)
+    )
+    queries, keys, values, share = lax.optimization_barrier((queries, keys, values, share))
+    zh = lax.axis_index("zh")
+    other = lax.ppermute(share, "zh", [(0, 1), (1, 0), (2, 3), (3, 2)])
+    pair = jnp.where(zh % 2 == 0, jnp.stack([share, other]), jnp.stack([other, share]))
+    rest = lax.ppermute(pair, "zh", [(1, 2), (2, 1), (3, 0), (0, 3)])
+    packed, rest = lax.optimization_barrier((pack(queries[0], keys[0], values[0]), rest))
+    qkv = lax.all_to_all(packed, SEQ, 0, 0, tiled=True)
+    share = jnp.where(zh < 2, jnp.concatenate([pair, rest]), jnp.concatenate([rest, pair]))
+    share = lax.all_gather(share, "y")
+    share = share.transpose(1, 0, 2, 3).reshape(BLOCK, WIDTH // 2)
+    near = [share]
+    for shift in (1, 2, 3):
+        near.append(lax.ppermute(share, "x", [(i, (i + shift) % 4) for i in range(4)]))
+
     edge = jnp.concatenate([frames[0, -EDGE:], cotangent[0, -16:]], axis=0)
     forward_pairs = [(i, i + 1) for i in range(HEADS - 1)]
     low = lax.ppermute(edge, SEQ, forward_pairs)
@@ -382,11 +418,16 @@
     taps = conv_kernel.reshape(KERNEL, 1, TILES, LANES)
     taps = jnp.concatenate([taps, taps], axis=1).reshape(KERNEL * GROUP, LANES)
 
-    heads, wide_frames, wide_cot, taps = lax.optimization_barrier(
-        (attend(lengths, qkv), wide_frames, wide_cot, taps)
+    swap = [(0, 1), (1, 0)]
+    far = [lax.ppermute(share, "c", swap)]
+    qkv, far, wide_frames, wide_cot, taps = lax.optimization_barrier(
+        (qkv, far, wide_frames, wide_cot, taps)
     )
+    heads, near = lax.optimization_barrier((attend(lengths, qkv), near))
+    project = near + far + [lax.ppermute(block, "c", swap) for block in near[1:]]
+
     context = lax.all_to_all(heads, SEQ, 0, 0, tiled=True)
-    plain, grad, terms = forward(place, context, project, wide_frames, wide_cot, taps)
+    plain, grad, terms = forward(place, context, wide_frames, wide_cot, taps, project)
 
     near_axes = ("zl", "y", "c")
     part = jnp.sum(lax.all_to_all(terms, near_axes, 0, 0, tiled=True), axis=0)

time: 234 us -> 216 us (0.923)
  waiting for transfers between devices: 88 us -> 25.5 us
  blocking collectives: 36.4 us -> 66.6 us
  starting transfers between devices: 42 us -> 66.5 us
  between operations: 14.9 us -> 1.6 us
  other arithmetic: 1.63 us -> 4.43 us
  Pallas kernels: 42.4 us -> 45.1 us
  local copies, waits for them, and re-layouts: 7.61 us -> 5.07 us
    all_to_all x1, waiting for transfers between devices: 39 us -> 0.01 us  [local(): qkv = lax.all_to_all(packed, SEQ, 0, 0, tiled=True)]
    all_gather x1 -> x0, waiting for transfers between devices: 36.7 us -> none  [local(): project = lax.all_gather(out_proj.T, DP, axis=0, tiled=True)]
    ppermute x0 -> x9, starting transfers between devices: none -> 36.3 us  [the longest x3 10.7 us: local(): lax.ppermute(share, 'x', [(i, (i + shift) % 4) for i in range(4)])]
    all_gather x0 -> x2, blocking collectives: none -> 30.1 us  [the longest x1 21.3 us: local(): share = lax.all_gather(share, 'y')]
    all_to_all x1, starting transfers between devices: 16.1 us -> 4.29 us  [local(): context = lax.all_to_all(heads, SEQ, 0, 0, tiled=True)]
    ppermute x0 -> x9, waiting for transfers between devices: none -> 9.59 us  [the longest x1 6.26 us: local(): other = lax.ppermute(share, 'zh', [(0, 1), (1, 0), (2, 3), (3, 2)])]
    unnamed x16 -> x10, local copies, waits for them, and re-layouts: 5.92 us -> 1.65 us
    all_to_all x1, waiting for transfers between devices: 4.83 us -> 7.3 us  [spread(): return lax.all_to_all(copies, axes, 0, 0, tiled=True)]
  transfers between devices with their start and end apart: 6 -> 14, of which waited for: 4 -> 6; matrix products, arithmetic and copies ran while one was open for 1% -> 2% of each run, Pallas kernels for 11% -> 14%
where the time goes in v2:
time: 216 us; the launch traced here: 215 us
  blocking collectives  66.6 us (31%)
  starting transfers between devices  66.5 us (31%)
  Pallas kernels  45.1 us (21%)
  waiting for transfers between devices  25.5 us (12%)
  local copies, waits for them, and re-layouts  5.07 us (2%)
  other arithmetic  4.43 us (2%)
    all_gather x1, blocking collectives, local(): share = lax.all_gather(share, 'y')  21.3 us
    all_to_all x1, blocking collectives, local(): part = jnp.sum(lax.all_to_all(terms, near_axes, 0, 0, tiled=True), axis=0)  19.4 us
    pallas_call x1, Pallas kernels, attend(): pl.pallas_call(attend_kernel, in_specs=[pl.BlockSpec(memory_space=pltpu.S...  17.3 us
    all_to_all x1, blocking collectives, spread(): return lax.all_to_all(copies, axes, 0, 0, tiled=True)  17.1 us
    pallas_call x1, Pallas kernels, forward(): pl.pallas_call(forward_kernel, in_specs=[pl.BlockSpec(memory_space=pltpu....  14.6 us
    all_to_all x1, starting transfers between devices, spread(): return lax.all_to_all(copies, axes, 0, 0, tiled=True)  12 us
    ppermute x3, starting transfers between devices, local(): lax.ppermute(share, 'x', [(i, (i + shift) % 4) for i in range(4)])  10.7 us
    ppermute x1, starting transfers between devices, local(): far = [lax.ppermute(share, 'c', swap)]  8.78 us
  transfers between devices with their start and end apart: 14, of which 6 were waited for; matrix products, arithmetic and copies ran while one was open for 2% of the time, Pallas kernels for 14%

profile of v2, /device:TPU:1, one launch (start us, length us, event | category | flops | bytes accessed | tf_op | source)
XLA Modules:
  0.0 214.8 jit_solution(4958529314117809321)
XLA Ops:
  0.6 8.7 %all_gather.7 = bf16[96,1536]{1,0:T(8,128)(2,1)S(1)} all-gather(bf16[48,1536]{1,0:T(8,128)(2,1)} %bitcast.46), channel_id=1, replica_groups=mesh['zl'=4,'y'=4,'x'=4,'zh'=4,'c'=2] {'c'}, dimensions={0}, use_global_device_ids=true | all-gather | bytes 442368 | tf_op jit(solution)/shard_map/all_gather | solution.py:392
  9.4 3.4 %collective-permute-start = (bf16[24,768]{1,0:T(8,128)(2,1)S(1)}, bf16[24,768]{1,0:T(8,128)(2,1)S(1)}, u32[]{:S(2)}, u32[]{:S(2)}) collective-permute-start(bf16[24,768]{1,0:T(8,128)(2,1)S(1)} %dynamic_slice.3), channel_id=1, source_target_pairs={{0,2},{2,0},{4,6},{6,4},{1,3},{3,1},{5,7},{7,5},{8,10},{10,8},{12,... | collective-permute-start | bytes 110600 | tf_op jit(solution)/shard_map/ppermute | solution.py:399
  12.8 6.3 %collective-permute-done = bf16[24,768]{1,0:T(8,128)(2,1)S(1)} collective-permute-done((bf16[24,768]{1,0:T(8,128)(2,1)S(1)}, bf16[24,768]{1,0:T(8,128)(2,1)S(1)}, u32[]{:S(2)}, u32[]{:S(2)}) %collective-permute-start) | collective-permute-done | bytes 36896 | tf_op jit(solution)/shard_map/ppermute | solution.py:399
  19.1 6.1 %collective-permute-start.1 = (bf16[2,24,768]{2,1,0:T(8,128)(2,1)S(1)}, bf16[2,24,768]{2,1,0:T(8,128)(2,1)S(1)}, u32[]{:S(2)}, u32[]{:S(2)}) collective-permute-start(bf16[2,24,768]{2,1,0:T(8,128)(2,1)S(1)} %maximum_select_fusion.1), channel_id=1, source_target_pairs={{2,4},{4,2},{6,0},{0,6},{3,5},{5,3},{7,1},{1,7},{10,12},{12,10},{1... | collective-permute-start | bytes 221192 | tf_op jit(solution)/shard_map/ppermute | solution.py:401
  25.2 4.5 %pack.1 = bf16[16,3,144,128]{3,2,1,0:T(8,128)(2,1)} custom-call(bf16[192,1536]{1,0:T(8,128)(2,1)} %bitcast.40, bf16[192,1536]{1,0:T(8,128)(2,1)} %bitcast.41, bf16[192,1536]{1,0:T(8,128)(2,1)} %bitcast.42), custom_call_target="tpu_custom_call" | custom-call | bytes 4000000 | tf_op jit(solution)/shard_map/pack/pallas_call | solution.py:59
  29.7 8.0 %all-to-all-start = ((bf16[16,3,144,128]{3,2,1,0:T(8,128)(2,1)}), bf16[16,3,144,128]{3,2,1,0:T(8,128)(2,1)}, u32[]{:S(2)}, u32[]{:S(2)}) async-start(bf16[16,3,144,128]{3,2,1,0:T(8,128)(2,1)} %pack.1), calls=%async_computation | async-start | bytes 3538944 | tf_op jit(solution)/shard_map/all_to_all | solution.py:403
  39.3 1.3 collective-permute-start.4
  41.2 4.6 %collective-permute-start.3 = (bf16[48,1536]{1,0:T(8,128)(2,1)}, bf16[48,1536]{1,0:T(8,128)(2,1)}, u32[]{:S(2)}, u32[]{:S(2)}) collective-permute-start(bf16[48,1536]{1,0:T(8,128)(2,1)} %pad_maximum_fusion.3), channel_id=1, source_target_pairs={{0,32},{32,64},{64,96},{96,128},{128,160},{160,192},{192,224},{224... | collective-permute-start | bytes 442376 | tf_op jit(solution)/shard_map/ppermute | solution.py:413
  46.6 21.3 %all_gather.8 = bf16[4,4,24,768]{3,2,1,0:T(8,128)(2,1)S(1)} all-gather(bf16[1,4,24,768]{3,2,1,0:T(8,128)(2,1)S(1)} %maximum_select_fusion), channel_id=1, replica_groups=mesh['zl'=4,'y'=4,'x'=4,'zh'=4,'c'=2] {'y'}, dimensions={0}, use_global_device_ids=true | all-gather | bytes 737280 | tf_op jit(solution)/shard_map/all_gather | solution.py:405
  68.0 8.8 %collective-permute-start.2 = (bf16[384,768]{1,0:T(8,128)(2,1)S(1)}, bf16[384,768]{1,0:T(8,128)(2,1)S(1)}, u32[]{:S(2)}, u32[]{:S(2)}) collective-permute-start(bf16[384,768]{1,0:T(8,128)(2,1)S(1)} %bitcast.30), channel_id=1, source_target_pairs={{0,1},{1,0},{2,3},{3,2},{4,5},{5,4},{6,7},{7,6},{8,9},{9,8},{10,11... | collective-permute-start | bytes 1769480 | tf_op jit(solution)/shard_map/ppermute | solution.py:422
  77.0 3.3 %collective-permute-start.5 = (bf16[384,768]{1,0:T(8,128)(2,1)S(1)}, bf16[384,768]{1,0:T(8,128)(2,1)S(1)}, u32[]{:S(2)}, u32[]{:S(2)}) collective-permute-start(bf16[384,768]{1,0:T(8,128)(2,1)S(1)} %bitcast.31), channel_id=1, source_target_pairs={{0,8},{8,16},{16,24},{24,0},{1,9},{9,17},{17,25},{25,1},{2,10},{10... | collective-permute-start | bytes 1769480 | tf_op jit(solution)/shard_map/ppermute | solution.py:409
  80.2 4.4 %collective-permute-start.6 = (bf16[384,768]{1,0:T(8,128)(2,1)S(1)}, bf16[384,768]{1,0:T(8,128)(2,1)S(1)}, u32[]{:S(2)}, u32[]{:S(2)}) collective-permute-start(bf16[384,768]{1,0:T(8,128)(2,1)S(1)} %bitcast.32), channel_id=1, source_target_pairs={{0,16},{8,24},{16,0},{24,8},{1,17},{9,25},{17,1},{25,9},{2,18},{10... | collective-permute-start | bytes 1769480 | tf_op jit(solution)/shard_map/ppermute | solution.py:409
  84.6 3.1 %collective-permute-start.7 = (bf16[384,768]{1,0:T(8,128)(2,1)S(1)}, bf16[384,768]{1,0:T(8,128)(2,1)}, u32[]{:S(2)}, u32[]{:S(2)}) collective-permute-start(bf16[384,768]{1,0:T(8,128)(2,1)S(1)} %bitcast.33), channel_id=1, source_target_pairs={{0,24},{8,0},{16,8},{24,16},{1,25},{9,1},{17,9},{25,17},{2,26},{10... | collective-permute-start | bytes 1769480 | tf_op jit(solution)/shard_map/ppermute | solution.py:409
  87.7 0.9 slice.36
  89.4 0.9 pad_maximum_fusion.frames_ref
  90.4 17.3 %attend.1 = bf16[16,192,128]{2,1,0:T(8,128)(2,1)S(1)} custom-call(s32[1]{0:T(128)S(6)} %copy.22.length_ref, bf16[16,3,144,128]{3,2,1,0:T(8,128)(2,1)} %all-to-all-done.qkv_ref), custom_call_target="tpu_custom_call" | custom-call | flops 4831838208 | bytes 3000000 | tf_op jit(solution)/shard_map/attend/pallas_call | solution.py:160
  107.8 0.9 copy-done
  108.8 1.3 collective-permute-done.7.refs_3_
  110.1 4.3 %all-to-all-start.1 = ((bf16[16,192,128]{2,1,0:T(8,128)(2,1)}), bf16[16,192,128]{2,1,0:T(8,128)(2,1)}, u32[]{:S(2)}, u32[]{:S(2)}) async-start(bf16[16,192,128]{2,1,0:T(8,128)(2,1)} %copy-done), calls=%async_computation.1 | async-start | bytes 1572864 | tf_op jit(solution)/shard_map/all_to_all | solution.py:429
  114.4 3.0 %collective-permute-start.8 = (bf16[384,768]{1,0:T(8,128)(2,1)S(1)}, bf16[384,768]{1,0:T(8,128)(2,1)}, u32[]{:S(2)}, u32[]{:S(2)}) collective-permute-start(bf16[384,768]{1,0:T(8,128)(2,1)S(1)} %collective-permute-done.5.refs_1_), channel_id=1, source_target_pairs={{0,1},{1,0},{2,3},{3,2},{4,5},{5,4},{6,7},{7,6},{8,9},{9,8},{10,11... | collective-permute-start | bytes 1769480 | tf_op jit(solution)/shard_map/ppermute | solution.py:427
  117.4 1.9 collective-permute-start.9
  119.4 2.4 %collective-permute-start.10 = (bf16[384,768]{1,0:T(8,128)(2,1)}, bf16[384,768]{1,0:T(8,128)(2,1)}, u32[]{:S(2)}, u32[]{:S(2)}) collective-permute-start(bf16[384,768]{1,0:T(8,128)(2,1)} %collective-permute-done.7.refs_3_), channel_id=1, source_target_pairs={{0,1},{1,0},{2,3},{3,2},{4,5},{5,4},{6,7},{7,6},{8,9},{9,8},{10,11... | collective-permute-start | bytes 1769480 | tf_op jit(solution)/shard_map/ppermute | solution.py:427
  121.9 1.9 collective-permute-done.10.refs_7_
  123.7 8.6 %all-to-all-done.1.context_ref = bf16[16,192,128]{2,1,0:T(8,128)(2,1)} async-done(((bf16[16,192,128]{2,1,0:T(8,128)(2,1)}), bf16[16,192,128]{2,1,0:T(8,128)(2,1)}, u32[]{:S(2)}, u32[]{:S(2)}) %all-to-all-start.1) | async-done | bytes 786464 | tf_op jit(solution)/shard_map/all_to_all | solution.py:429
  132.3 14.6 %forward.1 = (f32[3072,128]{1,0:T(8,128)}, f32[3072,128]{1,0:T(8,128)}, f32[32,16,128]{2,1,0:T(8,128)S(1)}) custom-call(s32[4]{0:T(128)S(1)} %pad_add_fusion.place_ref, bf16[16,192,128]{2,1,0:T(8,128)(2,1)} %all-to-all-done.1.context_ref, bf16[256,1536]{1,0:T(8,128)(2,1)} %pad_maximum_fusion.frames_ref, bf16[224,1536]{1,0:T(8,128)(2,1)S(1)} %pad_maximum_fusion.1.cot_ref, ...), custom_call_target="tpu_custom_call" | custom-call | flops 1207959552 | bytes 10000000 | tf_op jit(solution)/shard_map/forward/pallas_call | solution.py:297
  147.0 19.4 %all_to_all.25 = f32[32,16,128]{2,1,0:T(8,128)} all-to-all(f32[32,16,128]{2,1,0:T(8,128)S(1)} %get-tuple-element.44), channel_id=1, replica_groups=mesh['zl'=4,'y'=4,'x'=4,'zh'=4,'c'=2] {'zl','y','c'}, dimensions={0} | all-to-all | bytes 524288 | tf_op jit(solution)/shard_map/all_to_all | solution.py:433
  166.4 1.0 reduce_sum.18
  168.0 12.0 %all-to-all-start.3 = ((f32[16,16,128]{2,1,0:T(8,128)}), f32[16,16,128]{2,1,0:T(8,128)}, u32[]{:S(2)}, u32[]{:S(2)}) async-start(f32[16,16,128]{2,1,0:T(8,128)} %broadcast_in_dim.10), calls=%async_computation.3 | async-start | bytes 262144 | tf_op jit(solution)/shard_map/all_to_all | solution.py:384
  180.0 8.6 %backward.1 = (bf16[192,1536]{1,0:T(8,128)(2,1)}, bf16[192,1536]{1,0:T(8,128)(2,1)}, bf16[192,1536]{1,0:T(8,128)(2,1)}) custom-call(s32[4]{0:T(128)S(1)} %pad_add_fusion.place_ref, f32[3072,128]{1,0:T(8,128)} %get-tuple-element.45.plain_ref, f32[3072,128]{1,0:T(8,128)} %get-tuple-element.46.grad_ref, bf16[224,1536]{1,0:T(8,128)(2,1)S(1)} %pad_maximum_fusion.1.cot_ref, ...), custom_call_target="tpu_custom_call" | custom-call | flops 905969664 | bytes 12000000 | tf_op jit(solution)/shard_map/backward/pallas_call | solution.py:368
  188.6 7.3 %all-to-all-done.3 = f32[16,16,128]{2,1,0:T(8,128)} async-done(((f32[16,16,128]{2,1,0:T(8,128)}), f32[16,16,128]{2,1,0:T(8,128)}, u32[]{:S(2)}, u32[]{:S(2)}) %all-to-all-start.3) | async-done | bytes 131104 | tf_op jit(solution)/shard_map/all_to_all | solution.py:384
  195.9 0.9 reduce_sum.19
  196.9 17.1 %all_to_all.26 = f32[32,16,128]{2,1,0:T(8,128)S(1)} all-to-all(f32[32,16,128]{2,1,0:T(8,128)S(1)} %broadcast_in_dim.25), channel_id=1, replica_groups=mesh['zl'=4,'y'=4,'x'=4,'zh'=4,'c'=2] {'zl','y','c'}, dimensions={0} | all-to-all | bytes 524288 | tf_op jit(solution)/shard_map/all_to_all | solution.py:384
  (39 shorter events, 5.0 us)
Async XLA Ops:
  9.4 9.7 %collective-permute-start = (bf16[24,768]{1,0:T(8,128)(2,1)S(1)}, bf16[24,768]{1,0:T(8,128)(2,1)S(1)}, u32[]{:S(2)}, u32[]{:S(2)}) collective-permute-start(bf16[24,768]{1,0:T(8,128)(2,1)S(1)} %dynamic_slice.3), channel_id=1, source_target_pairs={{0,2},{2,0},{4,6},{6,4},{1,3},{3,1},{5,7},{7,5},{8,10},{10,8},{12,... | collective-permute-start | bytes 110600 | tf_op jit(solution)/shard_map/ppermute | solution.py:399
  19.1 10.6 %collective-permute-start.1 = (bf16[2,24,768]{2,1,0:T(8,128)(2,1)S(1)}, bf16[2,24,768]{2,1,0:T(8,128)(2,1)S(1)}, u32[]{:S(2)}, u32[]{:S(2)}) collective-permute-start(bf16[2,24,768]{2,1,0:T(8,128)(2,1)S(1)} %maximum_select_fusion.1), channel_id=1, source_target_pairs={{2,4},{4,2},{6,0},{0,6},{3,5},{5,3},{7,1},{1,7},{10,12},{12,10},{1... | collective-permute-start | bytes 221192 | tf_op jit(solution)/shard_map/ppermute | solution.py:401
  29.7 8.9 %copy-start.1 = (bf16[1,192,1536]{2,1,0:T(8,128)(2,1)S(1)}, bf16[1,192,1536]{2,1,0:T(8,128)(2,1)}, u32[]{:S(2)}) copy-start(bf16[1,192,1536]{2,1,0:T(8,128)(2,1)} %param.8) | copy-start | bytes 1769476
  29.7 16.8 %copy-start.3 = (f32[31,1536]{1,0:T(8,128)S(1)}, f32[31,1536]{1,0:T(8,128)}, u32[]{:S(2)}) copy-start(f32[31,1536]{1,0:T(8,128)} %param.14) | copy-start | bytes 571396
  29.7 60.7 %all-to-all-start = ((bf16[16,3,144,128]{3,2,1,0:T(8,128)(2,1)}), bf16[16,3,144,128]{3,2,1,0:T(8,128)(2,1)}, u32[]{:S(2)}, u32[]{:S(2)}) async-start(bf16[16,3,144,128]{3,2,1,0:T(8,128)(2,1)} %pack.1), calls=%async_computation | async-start | bytes 3538944 | tf_op jit(solution)/shard_map/all_to_all | solution.py:403
  39.3 45.3 %collective-permute-start.4 = (bf16[48,1536]{1,0:T(8,128)(2,1)}, bf16[48,1536]{1,0:T(8,128)(2,1)S(1)}, u32[]{:S(2)}, u32[]{:S(2)}) collective-permute-start(bf16[48,1536]{1,0:T(8,128)(2,1)} %pad_maximum_fusion.4), channel_id=1, source_target_pairs={{32,0},{64,32},{96,64},{128,96},{160,128},{192,160},{224,192},{256... | collective-permute-start | bytes 442376 | tf_op jit(solution)/shard_map/ppermute | solution.py:415
  41.2 46.5 %collective-permute-start.3 = (bf16[48,1536]{1,0:T(8,128)(2,1)}, bf16[48,1536]{1,0:T(8,128)(2,1)}, u32[]{:S(2)}, u32[]{:S(2)}) collective-permute-start(bf16[48,1536]{1,0:T(8,128)(2,1)} %pad_maximum_fusion.3), channel_id=1, source_target_pairs={{0,32},{32,64},{64,96},{96,128},{128,160},{160,192},{192,224},{224... | collective-permute-start | bytes 442376 | tf_op jit(solution)/shard_map/ppermute | solution.py:413
  68.0 22.4 %collective-permute-start.2 = (bf16[384,768]{1,0:T(8,128)(2,1)S(1)}, bf16[384,768]{1,0:T(8,128)(2,1)S(1)}, u32[]{:S(2)}, u32[]{:S(2)}) collective-permute-start(bf16[384,768]{1,0:T(8,128)(2,1)S(1)} %bitcast.30), channel_id=1, source_target_pairs={{0,1},{1,0},{2,3},{3,2},{4,5},{5,4},{6,7},{7,6},{8,9},{9,8},{10,11... | collective-permute-start | bytes 1769480 | tf_op jit(solution)/shard_map/ppermute | solution.py:422
  77.0 13.4 %copy-start.2 = (bf16[1,192,1536]{2,1,0:T(8,128)(2,1)S(1)}, bf16[1,192,1536]{2,1,0:T(8,128)(2,1)}, u32[]{:S(2)}) copy-start(bf16[1,192,1536]{2,1,0:T(8,128)(2,1)} %param.15) | copy-start | bytes 1769476
  77.0 31.7 %collective-permute-start.5 = (bf16[384,768]{1,0:T(8,128)(2,1)S(1)}, bf16[384,768]{1,0:T(8,128)(2,1)S(1)}, u32[]{:S(2)}, u32[]{:S(2)}) collective-permute-start(bf16[384,768]{1,0:T(8,128)(2,1)S(1)} %bitcast.31), channel_id=1, source_target_pairs={{0,8},{8,16},{16,24},{24,0},{1,9},{9,17},{17,25},{25,1},{2,10},{10... | collective-permute-start | bytes 1769480 | tf_op jit(solution)/shard_map/ppermute | solution.py:409
  80.2 28.5 %collective-permute-start.6 = (bf16[384,768]{1,0:T(8,128)(2,1)S(1)}, bf16[384,768]{1,0:T(8,128)(2,1)S(1)}, u32[]{:S(2)}, u32[]{:S(2)}) collective-permute-start(bf16[384,768]{1,0:T(8,128)(2,1)S(1)} %bitcast.32), channel_id=1, source_target_pairs={{0,16},{8,24},{16,0},{24,8},{1,17},{9,25},{17,1},{25,9},{2,18},{10... | collective-permute-start | bytes 1769480 | tf_op jit(solution)/shard_map/ppermute | solution.py:409
  84.6 25.5 %collective-permute-start.7 = (bf16[384,768]{1,0:T(8,128)(2,1)S(1)}, bf16[384,768]{1,0:T(8,128)(2,1)}, u32[]{:S(2)}, u32[]{:S(2)}) collective-permute-start(bf16[384,768]{1,0:T(8,128)(2,1)S(1)} %bitcast.33), channel_id=1, source_target_pairs={{0,24},{8,0},{16,8},{24,16},{1,25},{9,1},{17,9},{25,17},{2,26},{10... | collective-permute-start | bytes 1769480 | tf_op jit(solution)/shard_map/ppermute | solution.py:409
  107.8 0.9 copy-start
  110.1 22.2 %all-to-all-start.1 = ((bf16[16,192,128]{2,1,0:T(8,128)(2,1)}), bf16[16,192,128]{2,1,0:T(8,128)(2,1)}, u32[]{:S(2)}, u32[]{:S(2)}) async-start(bf16[16,192,128]{2,1,0:T(8,128)(2,1)} %copy-done), calls=%async_computation.1 | async-start | bytes 1572864 | tf_op jit(solution)/shard_map/all_to_all | solution.py:429
  114.4 7.5 %collective-permute-start.8 = (bf16[384,768]{1,0:T(8,128)(2,1)S(1)}, bf16[384,768]{1,0:T(8,128)(2,1)}, u32[]{:S(2)}, u32[]{:S(2)}) collective-permute-start(bf16[384,768]{1,0:T(8,128)(2,1)S(1)} %collective-permute-done.5.refs_1_), channel_id=1, source_target_pairs={{0,1},{1,0},{2,3},{3,2},{4,5},{5,4},{6,7},{7,6},{8,9},{9,8},{10,11... | collective-permute-start | bytes 1769480 | tf_op jit(solution)/shard_map/ppermute | solution.py:427
  117.4 4.4 %collective-permute-start.9 = (bf16[384,768]{1,0:T(8,128)(2,1)S(1)}, bf16[384,768]{1,0:T(8,128)(2,1)}, u32[]{:S(2)}, u32[]{:S(2)}) collective-permute-start(bf16[384,768]{1,0:T(8,128)(2,1)S(1)} %collective-permute-done.6.refs_2_), channel_id=1, source_target_pairs={{0,1},{1,0},{2,3},{3,2},{4,5},{5,4},{6,7},{7,6},{8,9},{9,8},{10,11... | collective-permute-start | bytes 1769480 | tf_op jit(solution)/shard_map/ppermute | solution.py:427
  119.4 4.4 %collective-permute-start.10 = (bf16[384,768]{1,0:T(8,128)(2,1)}, bf16[384,768]{1,0:T(8,128)(2,1)}, u32[]{:S(2)}, u32[]{:S(2)}) collective-permute-start(bf16[384,768]{1,0:T(8,128)(2,1)} %collective-permute-done.7.refs_3_), channel_id=1, source_target_pairs={{0,1},{1,0},{2,3},{3,2},{4,5},{5,4},{6,7},{7,6},{8,9},{9,8},{10,11... | collective-permute-start | bytes 1769480 | tf_op jit(solution)/shard_map/ppermute | solution.py:427
  168.0 27.9 %all-to-all-start.3 = ((f32[16,16,128]{2,1,0:T(8,128)}), f32[16,16,128]{2,1,0:T(8,128)}, u32[]{:S(2)}, u32[]{:S(2)}) async-start(f32[16,16,128]{2,1,0:T(8,128)} %broadcast_in_dim.10), calls=%async_computation.3 | async-start | bytes 262144 | tf_op jit(solution)/shard_map/all_to_all | solution.py:384

commit v3 on v2

--- a/solution.py
+++ b/solution.py
@@ -21,7 +21,7 @@
 GROUP = 2 * TILES
 SLAB = 144
 EDGE = 32
-QUERY_ROWS = 2 * ROWS
+QUERY_ROWS = 4 * ROWS
 KEY_BLOCK = 512
 BF16 = jnp.bfloat16
 F32 = jnp.float32
@@ -408,6 +408,17 @@
     for shift in (1, 2, 3):
         near.append(lax.ppermute(share, "x", [(i, (i + shift) % 4) for i in range(4)]))
 
+    taps = conv_kernel.reshape(KERNEL, 1, TILES, LANES)
+    taps = jnp.concatenate([taps, taps], axis=1).reshape(KERNEL * GROUP, LANES)
+
+    swap = [(0, 1), (1, 0)]
+    far = [lax.ppermute(share, "c", swap)]
+    qkv, far, taps = lax.optimization_barrier((qkv, far, taps))
+    heads, near, frames, cotangent = lax.optimization_barrier(
+        (attend(lengths, qkv), near, frames, cotangent)
+    )
+    project = near + far + [lax.ppermute(block, "c", swap) for block in near[1:]]
+
     edge = jnp.concatenate([frames[0, -EDGE:], cotangent[0, -16:]], axis=0)
     forward_pairs = [(i, i + 1) for i in range(HEADS - 1)]
     low = lax.ppermute(edge, SEQ, forward_pairs)
@@ -415,16 +426,6 @@
     high = lax.ppermute(edge, SEQ, [(target, source) for source, target in forward_pairs])
     wide_frames = jnp.concatenate([low[:EDGE], frames[0], high[:EDGE]], axis=0)
     wide_cot = jnp.concatenate([low[EDGE:], cotangent[0], high[EDGE:]], axis=0)
-    taps = conv_kernel.reshape(KERNEL, 1, TILES, LANES)
-    taps = jnp.concatenate([taps, taps], axis=1).reshape(KERNEL * GROUP, LANES)
-
-    swap = [(0, 1), (1, 0)]
-    far = [lax.ppermute(share, "c", swap)]
-    qkv, far, wide_frames, wide_cot, taps = lax.optimization_barrier(
-        (qkv, far, wide_frames, wide_cot, taps)
-    )
-    heads, near = lax.optimization_barrier((attend(lengths, qkv), near))
-    project = near + far + [lax.ppermute(block, "c", swap) for block in near[1:]]
 
     context = lax.all_to_all(heads, SEQ, 0, 0, tiled=True)
     plain, grad, terms = forward(place, context, wide_frames, wide_cot, taps, project)

time: 216 us -> 215 us (level)
  waiting for transfers between devices: 25.5 us -> 16.4 us
  local copies, waits for them, and re-layouts: 5.07 us -> 12.3 us
  blocking collectives: 66.6 us -> 71.9 us
  starting transfers between devices: 66.5 us -> 64 us
  Pallas kernels: 45.1 us -> 42.7 us
    all_to_all x1, waiting for transfers between devices: 8.59 us -> 0.01 us  [local(): context = lax.all_to_all(heads, SEQ, 0, 0, tiled=True)]
    unnamed x10 -> x22, local copies, waits for them, and re-layouts: 1.65 us -> 9.59 us
    ppermute x1, starting transfers between devices: 8.78 us -> 4.47 us  [local(): far = [lax.ppermute(share, 'c', swap)]]
    all_to_all x1, blocking collectives: 19.4 us -> 23.6 us  [local(): part = jnp.sum(lax.all_to_all(terms, near_axes, 0, 0, tiled=True), axis=0)]
    ppermute x3, waiting for transfers between devices: 1.46 us -> 5.45 us  [local(): lax.ppermute(share, 'x', [(i, (i + shift) % 4) for i in range(4)])]
    all_to_all x1, waiting for transfers between devices: 7.3 us -> 4.65 us  [spread(): return lax.all_to_all(copies, axes, 0, 0, tiled=True)]
  transfers between devices with their start and end apart: 14 -> 14, of which waited for: 6 -> 4; matrix products, arithmetic and copies ran while one was open for 2% -> 2% of each run, Pallas kernels for 14% -> 13%
where the time goes in v3:
time: 215 us; the launch traced here: 214 us
  blocking collectives  71.9 us (33%)
  starting transfers between devices  64 us (30%)
  Pallas kernels  42.7 us (20%)
  waiting for transfers between devices  16.4 us (8%)
  local copies, waits for them, and re-layouts  12.3 us (6%)
  other arithmetic  5.23 us (2%)
    all_to_all x1, blocking collectives, local(): part = jnp.sum(lax.all_to_all(terms, near_axes, 0, 0, tiled=True), axis=0)  23.6 us
    all_gather x1, blocking collectives, local(): share = lax.all_gather(share, 'y')  22.4 us
    all_to_all x1, blocking collectives, spread(): return lax.all_to_all(copies, axes, 0, 0, tiled=True)  17.1 us
    pallas_call x1, Pallas kernels, attend(): pl.pallas_call(attend_kernel, in_specs=[pl.BlockSpec(memory_space=pltpu.S...  16.1 us
    pallas_call x1, Pallas kernels, forward(): pl.pallas_call(forward_kernel, in_specs=[pl.BlockSpec(memory_space=pltpu....  14 us
    all_to_all x1, starting transfers between devices, spread(): return lax.all_to_all(copies, axes, 0, 0, tiled=True)  11.8 us
    ppermute x3, starting transfers between devices, local(): lax.ppermute(share, 'x', [(i, (i + shift) % 4) for i in range(4)])  10.5 us
    unnamed x22, local copies, waits for them, and re-layouts  9.59 us
  transfers between devices with their start and end apart: 14, of which 4 were waited for; matrix products, arithmetic and copies ran while one was open for 2% of the time, Pallas kernels for 13%

profile of v3, /device:TPU:1, one launch (start us, length us, event | category | flops | bytes accessed | tf_op | source)
XLA Modules:
  0.0 214.1 jit_solution(2063756752487684271)
XLA Ops:
  0.6 8.7 %all_gather.7 = bf16[96,1536]{1,0:T(8,128)(2,1)S(1)} all-gather(bf16[48,1536]{1,0:T(8,128)(2,1)} %bitcast.46), channel_id=1, replica_groups=mesh['zl'=4,'y'=4,'x'=4,'zh'=4,'c'=2] {'c'}, dimensions={0}, use_global_device_ids=true | all-gather | bytes 442368 | tf_op jit(solution)/shard_map/all_gather | solution.py:392
  9.4 3.4 %collective-permute-start = (bf16[24,768]{1,0:T(8,128)(2,1)S(1)}, bf16[24,768]{1,0:T(8,128)(2,1)S(1)}, u32[]{:S(2)}, u32[]{:S(2)}) collective-permute-start(bf16[24,768]{1,0:T(8,128)(2,1)S(1)} %dynamic_slice.3), channel_id=1, source_target_pairs={{0,2},{2,0},{4,6},{6,4},{1,3},{3,1},{5,7},{7,5},{8,10},{10,8},{12,... | collective-permute-start | bytes 110600 | tf_op jit(solution)/shard_map/ppermute | solution.py:399
  12.8 6.3 %collective-permute-done = bf16[24,768]{1,0:T(8,128)(2,1)S(1)} collective-permute-done((bf16[24,768]{1,0:T(8,128)(2,1)S(1)}, bf16[24,768]{1,0:T(8,128)(2,1)S(1)}, u32[]{:S(2)}, u32[]{:S(2)}) %collective-permute-start) | collective-permute-done | bytes 36896 | tf_op jit(solution)/shard_map/ppermute | solution.py:399
  19.1 6.1 %collective-permute-start.1 = (bf16[2,24,768]{2,1,0:T(8,128)(2,1)S(1)}, bf16[2,24,768]{2,1,0:T(8,128)(2,1)S(1)}, u32[]{:S(2)}, u32[]{:S(2)}) collective-permute-start(bf16[2,24,768]{2,1,0:T(8,128)(2,1)S(1)} %maximum_select_fusion.1), channel_id=1, source_target_pairs={{2,4},{4,2},{6,0},{0,6},{3,5},{5,3},{7,1},{1,7},{10,12},{12,10},{1... | collective-permute-start | bytes 221192 | tf_op jit(solution)/shard_map/ppermute | solution.py:401
  25.2 4.5 %pack.1 = bf16[16,3,144,128]{3,2,1,0:T(8,128)(2,1)} custom-call(bf16[192,1536]{1,0:T(8,128)(2,1)} %bitcast.40, bf16[192,1536]{1,0:T(8,128)(2,1)} %bitcast.41, bf16[192,1536]{1,0:T(8,128)(2,1)} %bitcast.42), custom_call_target="tpu_custom_call" | custom-call | bytes 4000000 | tf_op jit(solution)/shard_map/pack/pallas_call | solution.py:59
  29.7 8.0 %all-to-all-start = ((bf16[16,3,144,128]{3,2,1,0:T(8,128)(2,1)}), bf16[16,3,144,128]{3,2,1,0:T(8,128)(2,1)}, u32[]{:S(2)}, u32[]{:S(2)}) async-start(bf16[16,3,144,128]{3,2,1,0:T(8,128)(2,1)} %pack.1), calls=%async_computation | async-start | bytes 3538944 | tf_op jit(solution)/shard_map/all_to_all | solution.py:403
  37.8 22.4 %all_gather.8 = bf16[4,4,24,768]{3,2,1,0:T(8,128)(2,1)S(1)} all-gather(bf16[1,4,24,768]{3,2,1,0:T(8,128)(2,1)S(1)} %maximum_select_fusion), channel_id=1, replica_groups=mesh['zl'=4,'y'=4,'x'=4,'zh'=4,'c'=2] {'y'}, dimensions={0}, use_global_device_ids=true | all-gather | bytes 737280 | tf_op jit(solution)/shard_map/all_gather | solution.py:405
  60.3 4.5 %collective-permute-start.2 = (bf16[384,768]{1,0:T(8,128)(2,1)S(1)}, bf16[384,768]{1,0:T(8,128)(2,1)S(1)}, u32[]{:S(2)}, u32[]{:S(2)}) collective-permute-start(bf16[384,768]{1,0:T(8,128)(2,1)S(1)} %bitcast.30), channel_id=1, source_target_pairs={{0,1},{1,0},{2,3},{3,2},{4,5},{5,4},{6,7},{7,6},{8,9},{9,8},{10,11... | collective-permute-start | bytes 1769480 | tf_op jit(solution)/shard_map/ppermute | solution.py:415
  64.7 3.1 %collective-permute-start.3 = (bf16[384,768]{1,0:T(8,128)(2,1)S(1)}, bf16[384,768]{1,0:T(8,128)(2,1)S(1)}, u32[]{:S(2)}, u32[]{:S(2)}) collective-permute-start(bf16[384,768]{1,0:T(8,128)(2,1)S(1)} %bitcast.31), channel_id=1, source_target_pairs={{0,8},{8,16},{16,24},{24,0},{1,9},{9,17},{17,25},{25,1},{2,10},{10... | collective-permute-start | bytes 1769480 | tf_op jit(solution)/shard_map/ppermute | solution.py:409
  67.9 4.4 %collective-permute-start.4 = (bf16[384,768]{1,0:T(8,128)(2,1)S(1)}, bf16[384,768]{1,0:T(8,128)(2,1)S(1)}, u32[]{:S(2)}, u32[]{:S(2)}) collective-permute-start(bf16[384,768]{1,0:T(8,128)(2,1)S(1)} %bitcast.32), channel_id=1, source_target_pairs={{0,16},{8,24},{16,0},{24,8},{1,17},{9,25},{17,1},{25,9},{2,18},{10... | collective-permute-start | bytes 1769480 | tf_op jit(solution)/shard_map/ppermute | solution.py:409
  72.2 3.1 %collective-permute-start.5 = (bf16[384,768]{1,0:T(8,128)(2,1)S(1)}, bf16[384,768]{1,0:T(8,128)(2,1)}, u32[]{:S(2)}, u32[]{:S(2)}) collective-permute-start(bf16[384,768]{1,0:T(8,128)(2,1)S(1)} %bitcast.33), channel_id=1, source_target_pairs={{0,24},{8,0},{16,8},{24,16},{1,25},{9,1},{17,9},{25,17},{2,26},{10... | collective-permute-start | bytes 1769480 | tf_op jit(solution)/shard_map/ppermute | solution.py:409
  76.2 16.1 %attend.1 = bf16[16,192,128]{2,1,0:T(8,128)(2,1)} custom-call(s32[1]{0:T(128)S(6)} %copy.22.length_ref, bf16[16,3,144,128]{3,2,1,0:T(8,128)(2,1)} %all-to-all-done.qkv_ref), custom_call_target="tpu_custom_call" | custom-call | flops 4831838208 | bytes 3000000 | tf_op jit(solution)/shard_map/attend/pallas_call | solution.py:160
  92.3 4.1 %collective-permute-done.4.refs_2_ = bf16[384,768]{1,0:T(8,128)(2,1)S(1)} collective-permute-done((bf16[384,768]{1,0:T(8,128)(2,1)S(1)}, bf16[384,768]{1,0:T(8,128)(2,1)S(1)}, u32[]{:S(2)}, u32[]{:S(2)}) %collective-permute-start.4) | collective-permute-done | bytes 589856 | tf_op jit(solution)/shard_map/ppermute | solution.py:409
  96.4 1.3 collective-permute-done.5.refs_3_
  97.8 6.0 %all-to-all-start.1 = ((bf16[16,192,128]{2,1,0:T(8,128)(2,1)}), bf16[16,192,128]{2,1,0:T(8,128)(2,1)}, u32[]{:S(2)}, u32[]{:S(2)}) async-start(bf16[16,192,128]{2,1,0:T(8,128)(2,1)} %attend.1), calls=%async_computation.1 | async-start | bytes 1572864 | tf_op jit(solution)/shard_map/all_to_all | solution.py:430
  105.6 1.3 collective-permute-start.7
  106.9 4.0 %collective-permute-start.6 = (bf16[48,1536]{1,0:T(8,128)(2,1)S(1)}, bf16[48,1536]{1,0:T(8,128)(2,1)S(1)}, u32[]{:S(2)}, u32[]{:S(2)}) collective-permute-start(bf16[48,1536]{1,0:T(8,128)(2,1)S(1)} %pad_maximum_fusion.3), channel_id=1, source_target_pairs={{0,32},{32,64},{64,96},{96,128},{128,160},{160,192},{192,224},{224... | collective-permute-start | bytes 442376 | tf_op jit(solution)/shard_map/ppermute | solution.py:424
  110.9 3.9 %collective-permute-start.8 = (bf16[384,768]{1,0:T(8,128)(2,1)S(1)}, bf16[384,768]{1,0:T(8,128)(2,1)S(1)}, u32[]{:S(2)}, u32[]{:S(2)}) collective-permute-start(bf16[384,768]{1,0:T(8,128)(2,1)S(1)} %collective-permute-done.3.refs_1_), channel_id=1, source_target_pairs={{0,1},{1,0},{2,3},{3,2},{4,5},{5,4},{6,7},{7,6},{8,9},{9,8},{10,11... | collective-permute-start | bytes 1769480 | tf_op jit(solution)/shard_map/ppermute | solution.py:420
  114.8 2.1 collective-permute-start.9
  116.9 2.4 %collective-permute-start.10 = (bf16[384,768]{1,0:T(8,128)(2,1)}, bf16[384,768]{1,0:T(8,128)(2,1)S(1)}, u32[]{:S(2)}, u32[]{:S(2)}) collective-permute-start(bf16[384,768]{1,0:T(8,128)(2,1)} %collective-permute-done.5.refs_3_), channel_id=1, source_target_pairs={{0,1},{1,0},{2,3},{3,2},{4,5},{5,4},{6,7},{7,6},{8,9},{9,8},{10,11... | collective-permute-start | bytes 1769480 | tf_op jit(solution)/shard_map/ppermute | solution.py:420
  119.5 1.1 pad_maximum_fusion.1.cot_ref
  120.6 2.0 pad_maximum_fusion.frames_ref
  125.0 1.1 copy-done.1
  126.1 1.1 copy-done.4
  127.2 1.1 copy-done.7
  128.2 14.0 %forward.1 = (f32[3072,128]{1,0:T(8,128)}, f32[3072,128]{1,0:T(8,128)}, f32[32,16,128]{2,1,0:T(8,128)S(1)}) custom-call(s32[4]{0:T(128)S(1)} %pad_add_fusion.place_ref, bf16[16,192,128]{2,1,0:T(8,128)(2,1)} %all-to-all-done.1.context_ref, bf16[256,1536]{1,0:T(8,128)(2,1)} %pad_maximum_fusion.frames_ref, bf16[224,1536]{1,0:T(8,128)(2,1)S(1)} %pad_maximum_fusion.1.cot_ref, ...), custom_call_target="tpu_custom_call" | custom-call | flops 1207959552 | bytes 10000000 | tf_op jit(solution)/shard_map/forward/pallas_call | solution.py:297
  142.3 23.6 %all_to_all.25 = f32[32,16,128]{2,1,0:T(8,128)} all-to-all(f32[32,16,128]{2,1,0:T(8,128)S(1)} %get-tuple-element.44), channel_id=1, replica_groups=mesh['zl'=4,'y'=4,'x'=4,'zh'=4,'c'=2] {'zl','y','c'}, dimensions={0} | all-to-all | bytes 524288 | tf_op jit(solution)/shard_map/all_to_all | solution.py:434
  167.5 11.8 %all-to-all-start.3 = ((f32[16,16,128]{2,1,0:T(8,128)}), f32[16,16,128]{2,1,0:T(8,128)}, u32[]{:S(2)}, u32[]{:S(2)}) async-start(f32[16,16,128]{2,1,0:T(8,128)} %broadcast_in_dim.10), calls=%async_computation.3 | async-start | bytes 262144 | tf_op jit(solution)/shard_map/all_to_all | solution.py:384
  180.4 1.1 copy-done.5
  182.6 8.1 %backward.1 = (bf16[192,1536]{1,0:T(8,128)(2,1)}, bf16[192,1536]{1,0:T(8,128)(2,1)}, bf16[192,1536]{1,0:T(8,128)(2,1)}) custom-call(s32[4]{0:T(128)S(1)} %pad_add_fusion.place_ref, f32[3072,128]{1,0:T(8,128)} %get-tuple-element.45.plain_ref, f32[3072,128]{1,0:T(8,128)} %get-tuple-element.46.grad_ref, bf16[224,1536]{1,0:T(8,128)(2,1)S(1)} %pad_maximum_fusion.1.cot_ref, ...), custom_call_target="tpu_custom_call" | custom-call | flops 905969664 | bytes 12000000 | tf_op jit(solution)/shard_map/backward/pallas_call | solution.py:368
  190.6 4.7 %all-to-all-done.3 = f32[16,16,128]{2,1,0:T(8,128)} async-done(((f32[16,16,128]{2,1,0:T(8,128)}), f32[16,16,128]{2,1,0:T(8,128)}, u32[]{:S(2)}, u32[]{:S(2)}) %all-to-all-start.3) | async-done | bytes 131104 | tf_op jit(solution)/shard_map/all_to_all | solution.py:384
  196.2 17.1 %all_to_all.26 = f32[32,16,128]{2,1,0:T(8,128)S(1)} all-to-all(f32[32,16,128]{2,1,0:T(8,128)S(1)} %broadcast_in_dim.25), channel_id=1, replica_groups=mesh['zl'=4,'y'=4,'x'=4,'zh'=4,'c'=2] {'zl','y','c'}, dimensions={0} | all-to-all | bytes 524288 | tf_op jit(solution)/shard_map/all_to_all | solution.py:384
  (51 shorter events, 10.2 us)
Async XLA Ops:
  9.4 9.7 %collective-permute-start = (bf16[24,768]{1,0:T(8,128)(2,1)S(1)}, bf16[24,768]{1,0:T(8,128)(2,1)S(1)}, u32[]{:S(2)}, u32[]{:S(2)}) collective-permute-start(bf16[24,768]{1,0:T(8,128)(2,1)S(1)} %dynamic_slice.3), channel_id=1, source_target_pairs={{0,2},{2,0},{4,6},{6,4},{1,3},{3,1},{5,7},{7,5},{8,10},{10,8},{12,... | collective-permute-start | bytes 110600 | tf_op jit(solution)/shard_map/ppermute | solution.py:399
  19.1 10.6 %collective-permute-start.1 = (bf16[2,24,768]{2,1,0:T(8,128)(2,1)S(1)}, bf16[2,24,768]{2,1,0:T(8,128)(2,1)S(1)}, u32[]{:S(2)}, u32[]{:S(2)}) collective-permute-start(bf16[2,24,768]{2,1,0:T(8,128)(2,1)S(1)} %maximum_select_fusion.1), channel_id=1, source_target_pairs={{2,4},{4,2},{6,0},{0,6},{3,5},{5,3},{7,1},{1,7},{10,12},{12,10},{1... | collective-permute-start | bytes 221192 | tf_op jit(solution)/shard_map/ppermute | solution.py:401
  29.7 46.5 %all-to-all-start = ((bf16[16,3,144,128]{3,2,1,0:T(8,128)(2,1)}), bf16[16,3,144,128]{3,2,1,0:T(8,128)(2,1)}, u32[]{:S(2)}, u32[]{:S(2)}) async-start(bf16[16,3,144,128]{3,2,1,0:T(8,128)(2,1)} %pack.1), calls=%async_computation | async-start | bytes 3538944 | tf_op jit(solution)/shard_map/all_to_all | solution.py:403
  37.7 38.2 %copy-start.9 = (f32[31,1536]{1,0:T(8,128)S(1)}, f32[31,1536]{1,0:T(8,128)}, u32[]{:S(2)}) copy-start(f32[31,1536]{1,0:T(8,128)} %param.14) | copy-start | bytes 571396
  60.3 15.9 %collective-permute-start.2 = (bf16[384,768]{1,0:T(8,128)(2,1)S(1)}, bf16[384,768]{1,0:T(8,128)(2,1)S(1)}, u32[]{:S(2)}, u32[]{:S(2)}) collective-permute-start(bf16[384,768]{1,0:T(8,128)(2,1)S(1)} %bitcast.30), channel_id=1, source_target_pairs={{0,1},{1,0},{2,3},{3,2},{4,5},{5,4},{6,7},{7,6},{8,9},{9,8},{10,11... | collective-permute-start | bytes 1769480 | tf_op jit(solution)/shard_map/ppermute | solution.py:415
  64.7 27.6 %collective-permute-start.3 = (bf16[384,768]{1,0:T(8,128)(2,1)S(1)}, bf16[384,768]{1,0:T(8,128)(2,1)S(1)}, u32[]{:S(2)}, u32[]{:S(2)}) collective-permute-start(bf16[384,768]{1,0:T(8,128)(2,1)S(1)} %bitcast.31), channel_id=1, source_target_pairs={{0,8},{8,16},{16,24},{24,0},{1,9},{9,17},{17,25},{25,1},{2,10},{10... | collective-permute-start | bytes 1769480 | tf_op jit(solution)/shard_map/ppermute | solution.py:409
  67.9 28.5 %collective-permute-start.4 = (bf16[384,768]{1,0:T(8,128)(2,1)S(1)}, bf16[384,768]{1,0:T(8,128)(2,1)S(1)}, u32[]{:S(2)}, u32[]{:S(2)}) collective-permute-start(bf16[384,768]{1,0:T(8,128)(2,1)S(1)} %bitcast.32), channel_id=1, source_target_pairs={{0,16},{8,24},{16,0},{24,8},{1,17},{9,25},{17,1},{25,9},{2,18},{10... | collective-permute-start | bytes 1769480 | tf_op jit(solution)/shard_map/ppermute | solution.py:409
  72.2 25.5 %collective-permute-start.5 = (bf16[384,768]{1,0:T(8,128)(2,1)S(1)}, bf16[384,768]{1,0:T(8,128)(2,1)}, u32[]{:S(2)}, u32[]{:S(2)}) collective-permute-start(bf16[384,768]{1,0:T(8,128)(2,1)S(1)} %bitcast.33), channel_id=1, source_target_pairs={{0,24},{8,0},{16,8},{24,16},{1,25},{9,1},{17,9},{25,17},{2,26},{10... | collective-permute-start | bytes 1769480 | tf_op jit(solution)/shard_map/ppermute | solution.py:409
  97.8 27.3 %all-to-all-start.1 = ((bf16[16,192,128]{2,1,0:T(8,128)(2,1)}), bf16[16,192,128]{2,1,0:T(8,128)(2,1)}, u32[]{:S(2)}, u32[]{:S(2)}) async-start(bf16[16,192,128]{2,1,0:T(8,128)(2,1)} %attend.1), calls=%async_computation.1 | async-start | bytes 1572864 | tf_op jit(solution)/shard_map/all_to_all | solution.py:430
  105.6 13.8 %collective-permute-start.7 = (bf16[48,1536]{1,0:T(8,128)(2,1)S(1)}, bf16[48,1536]{1,0:T(8,128)(2,1)S(1)}, u32[]{:S(2)}, u32[]{:S(2)}) collective-permute-start(bf16[48,1536]{1,0:T(8,128)(2,1)S(1)} %pad_maximum_fusion.4), channel_id=1, source_target_pairs={{32,0},{64,32},{96,64},{128,96},{160,128},{192,160},{224,192},{256... | collective-permute-start | bytes 442376 | tf_op jit(solution)/shard_map/ppermute | solution.py:426
  106.9 12.5 %collective-permute-start.6 = (bf16[48,1536]{1,0:T(8,128)(2,1)S(1)}, bf16[48,1536]{1,0:T(8,128)(2,1)S(1)}, u32[]{:S(2)}, u32[]{:S(2)}) collective-permute-start(bf16[48,1536]{1,0:T(8,128)(2,1)S(1)} %pad_maximum_fusion.3), channel_id=1, source_target_pairs={{0,32},{32,64},{64,96},{96,128},{128,160},{160,192},{192,224},{224... | collective-permute-start | bytes 442376 | tf_op jit(solution)/shard_map/ppermute | solution.py:424
  110.9 11.7 %collective-permute-start.8 = (bf16[384,768]{1,0:T(8,128)(2,1)S(1)}, bf16[384,768]{1,0:T(8,128)(2,1)S(1)}, u32[]{:S(2)}, u32[]{:S(2)}) collective-permute-start(bf16[384,768]{1,0:T(8,128)(2,1)S(1)} %collective-permute-done.3.refs_1_), channel_id=1, source_target_pairs={{0,1},{1,0},{2,3},{3,2},{4,5},{5,4},{6,7},{7,6},{8,9},{9,8},{10,11... | collective-permute-start | bytes 1769480 | tf_op jit(solution)/shard_map/ppermute | solution.py:420
  114.8 8.6 %collective-permute-start.9 = (bf16[384,768]{1,0:T(8,128)(2,1)S(1)}, bf16[384,768]{1,0:T(8,128)(2,1)S(1)}, u32[]{:S(2)}, u32[]{:S(2)}) collective-permute-start(bf16[384,768]{1,0:T(8,128)(2,1)S(1)} %collective-permute-done.4.refs_2_), channel_id=1, source_target_pairs={{0,1},{1,0},{2,3},{3,2},{4,5},{5,4},{6,7},{7,6},{8,9},{9,8},{10,11... | collective-permute-start | bytes 1769480 | tf_op jit(solution)/shard_map/ppermute | solution.py:420
  116.9 7.3 %collective-permute-start.10 = (bf16[384,768]{1,0:T(8,128)(2,1)}, bf16[384,768]{1,0:T(8,128)(2,1)S(1)}, u32[]{:S(2)}, u32[]{:S(2)}) collective-permute-start(bf16[384,768]{1,0:T(8,128)(2,1)} %collective-permute-done.5.refs_3_), channel_id=1, source_target_pairs={{0,1},{1,0},{2,3},{3,2},{4,5},{5,4},{6,7},{7,6},{8,9},{9,8},{10,11... | collective-permute-start | bytes 1769480 | tf_op jit(solution)/shard_map/ppermute | solution.py:420
  122.6 0.8 copy-start
  123.4 0.8 copy-start.3
  124.2 0.8 copy-start.6
  125.0 1.1 copy-start.1
  126.1 1.1 copy-start.4
  127.2 1.1 copy-start.7
  167.5 27.7 %all-to-all-start.3 = ((f32[16,16,128]{2,1,0:T(8,128)}), f32[16,16,128]{2,1,0:T(8,128)}, u32[]{:S(2)}, u32[]{:S(2)}) async-start(f32[16,16,128]{2,1,0:T(8,128)} %broadcast_in_dim.10), calls=%async_computation.3 | async-start | bytes 262144 | tf_op jit(solution)/shard_map/all_to_all | solution.py:384
  179.4 1.1 copy-start.2
  180.4 1.1 copy-start.5
  181.5 1.1 copy-start.8

commit v4 on v3

--- a/solution.py
+++ b/solution.py
@@ -210,7 +210,9 @@
     return ref[pl.ds(half * TILES + tile, HALF, stride=GROUP)]
 
 
-def forward_kernel(place_ref, context_ref, frames_ref, cot_ref, taps_ref, *refs):
+def forward_kernel(
+    place_ref, context_ref, low_ref, high_ref, frames_ref, cot_ref, taps_ref, *refs
+):
     project_refs, (plain_ref, grad_ref, terms_ref, dense, xs, hs, cs, both) = refs[:8], refs[8:]
     x, core, first, length = place_ref[0], place_ref[1], place_ref[2], place_ref[3]
     rows = ROWS + 2 * EDGE
@@ -235,8 +237,11 @@
     frame = first - EDGE + lax.broadcasted_iota(jnp.int32, (rows, LANES), 0)
     valid = (frame >= 0) & (frame < length)
     for tile in range(TILES):
-        block = cot_ref[:, tile * LANES : (tile + 1) * LANES].astype(F32)
-        to_steps(cs, block, 0, G_STEPS, tile)
+        columns = slice(tile * LANES, (tile + 1) * LANES)
+        block = jnp.concatenate(
+            [low_ref[EDGE:, columns], cot_ref[:, columns], high_ref[EDGE:, columns]], axis=0
+        )
+        to_steps(cs, block.astype(F32), 0, G_STEPS, tile)
     across = (((1,), (1,)), ((), ()))
     half_width = WIDTH // 2
     near = dense[:, pl.ds(pl.multiple_of(core * half_width, LANES), half_width)]
@@ -244,8 +249,11 @@
     for start, wide, near_ref, far_ref in project_blocks(x, project_refs):
         mixed = lax.dot_general(near, near_ref[...], across, preferred_element_type=F32)
         mixed += lax.dot_general(far, far_ref[...], across, preferred_element_type=F32)
-        columns = frames_ref[:, pl.ds(start, wide)]
-        hidden = (columns.astype(F32) + mixed).astype(BF16).astype(F32)
+        columns = pl.ds(start, wide)
+        stream = jnp.concatenate(
+            [low_ref[:EDGE, columns], frames_ref[:, columns], high_ref[:EDGE, columns]], axis=0
+        )
+        hidden = (stream.astype(F32) + mixed).astype(BF16).astype(F32)
         for i in range(wide // LANES):
             tile = start // LANES + i
             block = hidden[:, i * LANES : (i + 1) * LANES]
@@ -293,11 +301,11 @@
     terms_ref[:KERNEL, :TILES] = both[:, :TILES] + both[:, TILES:]
 
 
-def forward(place, context, frames, cotangent, taps, project):
+def forward(place, context, low, high, frames, cotangent, taps, project):
     return pl.pallas_call(
         forward_kernel,
         in_specs=[pl.BlockSpec(memory_space=pltpu.SMEM)]
-        + [pl.BlockSpec(memory_space=pltpu.VMEM)] * 12,
+        + [pl.BlockSpec(memory_space=pltpu.VMEM)] * 14,
         out_shape=[
             jax.ShapeDtypeStruct((G_STEPS * GROUP, LANES), F32),
             jax.ShapeDtypeStruct((G_STEPS * GROUP, LANES), F32),
@@ -315,7 +323,7 @@
             flops=2 * 256 * WIDTH * WIDTH, bytes_accessed=10_000_000, transcendentals=400_000
         ),
         name="forward",
-    )(place, context, frames, cotangent, taps, *project)
+    )(place, context, low, high, frames, cotangent, taps, *project)
 
 
 def backward_kernel(place_ref, plain_ref, grad_ref, cot_ref, taps_ref, *refs):
@@ -346,7 +354,7 @@
             plain = plain_ref[pl.ds(16 * GROUP + half * TILES + tile, HALF, stride=GROUP)]
             block_ref[rows, columns] = plain.astype(BF16)
             back = jnp.where(valid, from_steps(bs, half, tile), 0.0)
-            cot = cot_ref[16 + half * HALF : 16 + (half + 1) * HALF, columns].astype(F32)
+            cot = cot_ref[rows, columns].astype(F32)
             hidden_ref[rows, columns] = (cot + back).astype(BF16)
     half_width = WIDTH // 2
     blocks = [
@@ -424,16 +432,16 @@
     low = lax.ppermute(edge, SEQ, forward_pairs)
     edge = jnp.concatenate([frames[0, :EDGE], cotangent[0, :16]], axis=0)
     high = lax.ppermute(edge, SEQ, [(target, source) for source, target in forward_pairs])
-    wide_frames = jnp.concatenate([low[:EDGE], frames[0], high[:EDGE]], axis=0)
-    wide_cot = jnp.concatenate([low[EDGE:], cotangent[0], high[EDGE:]], axis=0)
 
     context = lax.all_to_all(heads, SEQ, 0, 0, tiled=True)
-    plain, grad, terms = forward(place, context, wide_frames, wide_cot, taps, project)
+    plain, grad, terms = forward(
+        place, context, low, high, frames[0], cotangent[0], taps, project
+    )
 
     near_axes = ("zl", "y", "c")
     part = jnp.sum(lax.all_to_all(terms, near_axes, 0, 0, tiled=True), axis=0)
     part = jnp.sum(spread(part, ("x", "zh")), axis=0)
-    block, hidden, grad_context = backward(place, plain, grad, wide_cot, taps, project)
+    block, hidden, grad_context = backward(place, plain, grad, cotangent[0], taps, project)
     part, block = lax.optimization_barrier((part, block))
     whole = spread(part, near_axes)[:KERNEL, :TILES].reshape(KERNEL, WIDTH)
     grad_kernel = whole / math.sqrt(LENGTH * 32)

time: 215 us -> 208 us (0.967)
  waiting for transfers between devices: 16.4 us -> 25.6 us
  local copies, waits for them, and re-layouts: 12.3 us -> 4.54 us
  blocking collectives: 71.9 us -> 67.5 us
  other arithmetic: 5.23 us -> 2.53 us
    unnamed x22 -> x10, local copies, waits for them, and re-layouts: 9.59 us -> 2.71 us
    ppermute x1, waiting for transfers between devices: 0.01 us -> 4.99 us  [local(): lax.ppermute(edge, SEQ, [(target, source) for source, target in forward_p...]
    all_to_all x1, blocking collectives: 23.6 us -> 19.2 us  [local(): part = jnp.sum(lax.all_to_all(terms, near_axes, 0, 0, tiled=True), axis=0)]
    concatenate x2 -> x0, other arithmetic: 3.11 us -> none  [the longest x1 2 us: local(): wide_frames = jnp.concatenate([low[:EDGE], frames[0], high[:EDGE]], axis=0)]
    all_to_all x1, waiting for transfers between devices: 4.65 us -> 7.26 us  [spread(): return lax.all_to_all(copies, axes, 0, 0, tiled=True)]
  transfers between devices with their start and end apart: 14 -> 14, of which waited for: 4 -> 6; matrix products, arithmetic and copies ran while one was open for 2% -> 1% of each run, Pallas kernels for 13% -> 14%
where the time goes in v4:
time: 208 us; the launch traced here: 207 us
  blocking collectives  67.5 us (32%)
  starting transfers between devices  62.7 us (30%)
  Pallas kernels  42.8 us (21%)
  waiting for transfers between devices  25.6 us (12%)
  local copies, waits for them, and re-layouts  4.54 us (2%)
  other arithmetic  2.53 us (1%)
    all_gather x1, blocking collectives, local(): share = lax.all_gather(share, 'y')  22.4 us
    all_to_all x1, blocking collectives, local(): part = jnp.sum(lax.all_to_all(terms, near_axes, 0, 0, tiled=True), axis=0)  19.2 us
    all_to_all x1, blocking collectives, spread(): return lax.all_to_all(copies, axes, 0, 0, tiled=True)  17.1 us
    pallas_call x1, Pallas kernels, attend(): pl.pallas_call(attend_kernel, in_specs=[pl.BlockSpec(memory_space=pltpu.S...  15.3 us
    pallas_call x1, Pallas kernels, forward(): pl.pallas_call(forward_kernel, in_specs=[pl.BlockSpec(memory_space=pltpu....  14.4 us
    all_to_all x1, starting transfers between devices, spread(): return lax.all_to_all(copies, axes, 0, 0, tiled=True)  11.6 us
    ppermute x3, starting transfers between devices, local(): lax.ppermute(share, 'x', [(i, (i + shift) % 4) for i in range(4)])  10.5 us
    all_gather x1, blocking collectives, local(): rows = lax.all_gather(out_proj.T, 'c', axis=0, tiled=True)  8.74 us
  transfers between devices with their start and end apart: 14, of which 6 were waited for; matrix products, arithmetic and copies ran while one was open for 1% of the time, Pallas kernels for 14%

profile of v4, /device:TPU:1, one launch (start us, length us, event | category | flops | bytes accessed | tf_op | source)
XLA Modules:
  0.0 207.2 jit_solution(6763295266925383719)
XLA Ops:
  0.6 8.7 %all_gather.7 = bf16[96,1536]{1,0:T(8,128)(2,1)S(1)} all-gather(bf16[48,1536]{1,0:T(8,128)(2,1)} %bitcast.47), channel_id=1, replica_groups=mesh['zl'=4,'y'=4,'x'=4,'zh'=4,'c'=2] {'c'}, dimensions={0}, use_global_device_ids=true | all-gather | bytes 442368 | tf_op jit(solution)/shard_map/all_gather | solution.py:400
  9.4 3.4 %collective-permute-start = (bf16[24,768]{1,0:T(8,128)(2,1)S(1)}, bf16[24,768]{1,0:T(8,128)(2,1)S(1)}, u32[]{:S(2)}, u32[]{:S(2)}) collective-permute-start(bf16[24,768]{1,0:T(8,128)(2,1)S(1)} %dynamic_slice.3), channel_id=1, source_target_pairs={{0,2},{2,0},{4,6},{6,4},{1,3},{3,1},{5,7},{7,5},{8,10},{10,8},{12,... | collective-permute-start | bytes 110600 | tf_op jit(solution)/shard_map/ppermute | solution.py:407
  12.8 6.3 %collective-permute-done = bf16[24,768]{1,0:T(8,128)(2,1)S(1)} collective-permute-done((bf16[24,768]{1,0:T(8,128)(2,1)S(1)}, bf16[24,768]{1,0:T(8,128)(2,1)S(1)}, u32[]{:S(2)}, u32[]{:S(2)}) %collective-permute-start) | collective-permute-done | bytes 36896 | tf_op jit(solution)/shard_map/ppermute | solution.py:407
  19.1 6.1 %collective-permute-start.1 = (bf16[2,24,768]{2,1,0:T(8,128)(2,1)S(1)}, bf16[2,24,768]{2,1,0:T(8,128)(2,1)S(1)}, u32[]{:S(2)}, u32[]{:S(2)}) collective-permute-start(bf16[2,24,768]{2,1,0:T(8,128)(2,1)S(1)} %maximum_select_fusion.1), channel_id=1, source_target_pairs={{2,4},{4,2},{6,0},{0,6},{3,5},{5,3},{7,1},{1,7},{10,12},{12,10},{1... | collective-permute-start | bytes 221192 | tf_op jit(solution)/shard_map/ppermute | solution.py:409
  25.2 4.5 %pack.1 = bf16[16,3,144,128]{3,2,1,0:T(8,128)(2,1)} custom-call(bf16[192,1536]{1,0:T(8,128)(2,1)} %bitcast.41, bf16[192,1536]{1,0:T(8,128)(2,1)} %bitcast.42, bf16[192,1536]{1,0:T(8,128)(2,1)} %bitcast.43), custom_call_target="tpu_custom_call" | custom-call | bytes 4000000 | tf_op jit(solution)/shard_map/pack/pallas_call | solution.py:59
  29.7 8.0 %all-to-all-start = ((bf16[16,3,144,128]{3,2,1,0:T(8,128)(2,1)}), bf16[16,3,144,128]{3,2,1,0:T(8,128)(2,1)}, u32[]{:S(2)}, u32[]{:S(2)}) async-start(bf16[16,3,144,128]{3,2,1,0:T(8,128)(2,1)} %pack.1), calls=%async_computation | async-start | bytes 3538944 | tf_op jit(solution)/shard_map/all_to_all | solution.py:411
  37.8 22.4 %all_gather.8 = bf16[4,4,24,768]{3,2,1,0:T(8,128)(2,1)S(1)} all-gather(bf16[1,4,24,768]{3,2,1,0:T(8,128)(2,1)S(1)} %maximum_select_fusion), channel_id=1, replica_groups=mesh['zl'=4,'y'=4,'x'=4,'zh'=4,'c'=2] {'y'}, dimensions={0}, use_global_device_ids=true | all-gather | bytes 737280 | tf_op jit(solution)/shard_map/all_gather | solution.py:413
  60.2 4.5 %collective-permute-start.2 = (bf16[384,768]{1,0:T(8,128)(2,1)S(1)}, bf16[384,768]{1,0:T(8,128)(2,1)S(1)}, u32[]{:S(2)}, u32[]{:S(2)}) collective-permute-start(bf16[384,768]{1,0:T(8,128)(2,1)S(1)} %bitcast.30), channel_id=1, source_target_pairs={{0,1},{1,0},{2,3},{3,2},{4,5},{5,4},{6,7},{7,6},{8,9},{9,8},{10,11... | collective-permute-start | bytes 1769480 | tf_op jit(solution)/shard_map/ppermute | solution.py:423
  64.7 3.1 %collective-permute-start.3 = (bf16[384,768]{1,0:T(8,128)(2,1)S(1)}, bf16[384,768]{1,0:T(8,128)(2,1)S(1)}, u32[]{:S(2)}, u32[]{:S(2)}) collective-permute-start(bf16[384,768]{1,0:T(8,128)(2,1)S(1)} %bitcast.31), channel_id=1, source_target_pairs={{0,8},{8,16},{16,24},{24,0},{1,9},{9,17},{17,25},{25,1},{2,10},{10... | collective-permute-start | bytes 1769480 | tf_op jit(solution)/shard_map/ppermute | solution.py:417
  67.9 4.4 %collective-permute-start.4 = (bf16[384,768]{1,0:T(8,128)(2,1)S(1)}, bf16[384,768]{1,0:T(8,128)(2,1)S(1)}, u32[]{:S(2)}, u32[]{:S(2)}) collective-permute-start(bf16[384,768]{1,0:T(8,128)(2,1)S(1)} %bitcast.32), channel_id=1, source_target_pairs={{0,16},{8,24},{16,0},{24,8},{1,17},{9,25},{17,1},{25,9},{2,18},{10... | collective-permute-start | bytes 1769480 | tf_op jit(solution)/shard_map/ppermute | solution.py:417
  72.2 3.1 %collective-permute-start.5 = (bf16[384,768]{1,0:T(8,128)(2,1)S(1)}, bf16[384,768]{1,0:T(8,128)(2,1)}, u32[]{:S(2)}, u32[]{:S(2)}) collective-permute-start(bf16[384,768]{1,0:T(8,128)(2,1)S(1)} %bitcast.33), channel_id=1, source_target_pairs={{0,24},{8,0},{16,8},{24,16},{1,25},{9,1},{17,9},{25,17},{2,26},{10... | collective-permute-start | bytes 1769480 | tf_op jit(solution)/shard_map/ppermute | solution.py:417
  76.2 15.3 %attend.1 = bf16[16,192,128]{2,1,0:T(8,128)(2,1)S(1)} custom-call(s32[1]{0:T(128)S(6)} %copy.22.length_ref, bf16[16,3,144,128]{3,2,1,0:T(8,128)(2,1)} %all-to-all-done.qkv_ref), custom_call_target="tpu_custom_call" | custom-call | flops 4831838208 | bytes 3000000 | tf_op jit(solution)/shard_map/attend/pallas_call | solution.py:160
  91.5 0.9 copy-done.2
  92.4 4.0 %collective-permute-done.4.refs_2_ = bf16[384,768]{1,0:T(8,128)(2,1)S(1)} collective-permute-done((bf16[384,768]{1,0:T(8,128)(2,1)S(1)}, bf16[384,768]{1,0:T(8,128)(2,1)S(1)}, u32[]{:S(2)}, u32[]{:S(2)}) %collective-permute-start.4) | collective-permute-done | bytes 589856 | tf_op jit(solution)/shard_map/ppermute | solution.py:417
  96.4 1.3 collective-permute-done.5.refs_3_
  97.8 6.0 %all-to-all-start.1 = ((bf16[16,192,128]{2,1,0:T(8,128)(2,1)}), bf16[16,192,128]{2,1,0:T(8,128)(2,1)}, u32[]{:S(2)}, u32[]{:S(2)}) async-start(bf16[16,192,128]{2,1,0:T(8,128)(2,1)} %copy-done.2), calls=%async_computation.1 | async-start | bytes 1572864 | tf_op jit(solution)/shard_map/all_to_all | solution.py:436
  103.8 3.3 %collective-permute-start.8 = (bf16[384,768]{1,0:T(8,128)(2,1)S(1)}, bf16[384,768]{1,0:T(8,128)(2,1)}, u32[]{:S(2)}, u32[]{:S(2)}) collective-permute-start(bf16[384,768]{1,0:T(8,128)(2,1)S(1)} %collective-permute-done.3.refs_1_), channel_id=1, source_target_pairs={{0,1},{1,0},{2,3},{3,2},{4,5},{5,4},{6,7},{7,6},{8,9},{9,8},{10,11... | collective-permute-start | bytes 1769480 | tf_op jit(solution)/shard_map/ppermute | solution.py:428
  107.1 1.9 collective-permute-start.9
  109.0 2.4 %collective-permute-start.10 = (bf16[384,768]{1,0:T(8,128)(2,1)}, bf16[384,768]{1,0:T(8,128)(2,1)}, u32[]{:S(2)}, u32[]{:S(2)}) collective-permute-start(bf16[384,768]{1,0:T(8,128)(2,1)} %collective-permute-done.5.refs_3_), channel_id=1, source_target_pairs={{0,1},{1,0},{2,3},{3,2},{4,5},{5,4},{6,7},{7,6},{8,9},{9,8},{10,11... | collective-permute-start | bytes 1769480 | tf_op jit(solution)/shard_map/ppermute | solution.py:428
  111.5 1.0 slice_bitcast_fusion
  113.1 3.5 %collective-permute-start.6 = (bf16[48,1536]{1,0:T(8,128)(2,1)}, bf16[48,1536]{1,0:T(8,128)(2,1)S(1)}, u32[]{:S(2)}, u32[]{:S(2)}) collective-permute-start(bf16[48,1536]{1,0:T(8,128)(2,1)} %pad_maximum_fusion.1), channel_id=1, source_target_pairs={{0,32},{32,64},{64,96},{96,128},{128,160},{160,192},{192,224},{224... | collective-permute-start | bytes 442376 | tf_op jit(solution)/shard_map/ppermute | solution.py:432
  117.3 1.5 collective-permute-start.7
  118.8 1.7 collective-permute-done.6.low_ref
  120.5 5.0 %collective-permute-done.7.high_ref = bf16[48,1536]{1,0:T(8,128)(2,1)} collective-permute-done((bf16[48,1536]{1,0:T(8,128)(2,1)}, bf16[48,1536]{1,0:T(8,128)(2,1)}, u32[]{:S(2)}, u32[]{:S(2)}) %collective-permute-start.7) | collective-permute-done | bytes 147488 | tf_op jit(solution)/shard_map/ppermute | solution.py:434
  125.5 1.1 copy-done.1
  126.6 14.4 %forward.1 = (f32[3072,128]{1,0:T(8,128)}, f32[3072,128]{1,0:T(8,128)}, f32[32,16,128]{2,1,0:T(8,128)S(1)}) custom-call(s32[4]{0:T(128)S(1)} %pad_add_fusion.place_ref, bf16[16,192,128]{2,1,0:T(8,128)(2,1)} %all-to-all-done.1.context_ref, bf16[48,1536]{1,0:T(8,128)(2,1)S(1)} %collective-permute-done.6.low_ref, ...), custom_call_target="tpu_custom_call" | custom-call | flops 1207959552 | bytes 10000000 | tf_op jit(solution)/shard_map/forward/pallas_call | solution.py:305
  140.9 19.2 %all_to_all.25 = f32[32,16,128]{2,1,0:T(8,128)} all-to-all(f32[32,16,128]{2,1,0:T(8,128)S(1)} %get-tuple-element.44), channel_id=1, replica_groups=mesh['zl'=4,'y'=4,'x'=4,'zh'=4,'c'=2] {'zl','y','c'}, dimensions={0} | all-to-all | bytes 524288 | tf_op jit(solution)/shard_map/all_to_all | solution.py:442
  160.2 1.0 reduce_sum.18
  161.8 11.6 %all-to-all-start.3 = ((f32[16,16,128]{2,1,0:T(8,128)}), f32[16,16,128]{2,1,0:T(8,128)S(1)}, u32[]{:S(2)}, u32[]{:S(2)}) async-start(f32[16,16,128]{2,1,0:T(8,128)} %broadcast_in_dim.10), calls=%async_computation.3 | async-start | bytes 262144 | tf_op jit(solution)/shard_map/all_to_all | solution.py:392
  173.4 8.6 %backward.1 = (bf16[192,1536]{1,0:T(8,128)(2,1)}, bf16[192,1536]{1,0:T(8,128)(2,1)}, bf16[192,1536]{1,0:T(8,128)(2,1)}) custom-call(s32[4]{0:T(128)S(1)} %pad_add_fusion.place_ref, f32[3072,128]{1,0:T(8,128)} %get-tuple-element.45.plain_ref, f32[3072,128]{1,0:T(8,128)} %get-tuple-element.46.grad_ref, bf16[192,1536]{1,0:T(8,128)(2,1)S(1)} %bitcast.37, ...), custom_call_target="tpu_custom_call" | custom-call | flops 905969664 | bytes 12000000 | tf_op jit(solution)/shard_map/backward/pallas_call | solution.py:376
  182.0 7.3 %all-to-all-done.3 = f32[16,16,128]{2,1,0:T(8,128)S(1)} async-done(((f32[16,16,128]{2,1,0:T(8,128)}), f32[16,16,128]{2,1,0:T(8,128)S(1)}, u32[]{:S(2)}, u32[]{:S(2)}) %all-to-all-start.3) | async-done | bytes 131104 | tf_op jit(solution)/shard_map/all_to_all | solution.py:392
  189.3 17.1 %all_to_all.26 = f32[32,16,128]{2,1,0:T(8,128)S(1)} all-to-all(f32[32,16,128]{2,1,0:T(8,128)S(1)} %broadcast_in_dim.25), channel_id=1, replica_groups=mesh['zl'=4,'y'=4,'x'=4,'zh'=4,'c'=2] {'zl','y','c'}, dimensions={0} | all-to-all | bytes 524288 | tf_op jit(solution)/shard_map/all_to_all | solution.py:392
  (33 shorter events, 3.2 us)
Async XLA Ops:
  9.4 9.7 %collective-permute-start = (bf16[24,768]{1,0:T(8,128)(2,1)S(1)}, bf16[24,768]{1,0:T(8,128)(2,1)S(1)}, u32[]{:S(2)}, u32[]{:S(2)}) collective-permute-start(bf16[24,768]{1,0:T(8,128)(2,1)S(1)} %dynamic_slice.3), channel_id=1, source_target_pairs={{0,2},{2,0},{4,6},{6,4},{1,3},{3,1},{5,7},{7,5},{8,10},{10,8},{12,... | collective-permute-start | bytes 110600 | tf_op jit(solution)/shard_map/ppermute | solution.py:407
  19.1 10.6 %collective-permute-start.1 = (bf16[2,24,768]{2,1,0:T(8,128)(2,1)S(1)}, bf16[2,24,768]{2,1,0:T(8,128)(2,1)S(1)}, u32[]{:S(2)}, u32[]{:S(2)}) collective-permute-start(bf16[2,24,768]{2,1,0:T(8,128)(2,1)S(1)} %maximum_select_fusion.1), channel_id=1, source_target_pairs={{2,4},{4,2},{6,0},{0,6},{3,5},{5,3},{7,1},{1,7},{10,12},{12,10},{1... | collective-permute-start | bytes 221192 | tf_op jit(solution)/shard_map/ppermute | solution.py:409
  29.7 46.5 %all-to-all-start = ((bf16[16,3,144,128]{3,2,1,0:T(8,128)(2,1)}), bf16[16,3,144,128]{3,2,1,0:T(8,128)(2,1)}, u32[]{:S(2)}, u32[]{:S(2)}) async-start(bf16[16,3,144,128]{3,2,1,0:T(8,128)(2,1)} %pack.1), calls=%async_computation | async-start | bytes 3538944 | tf_op jit(solution)/shard_map/all_to_all | solution.py:411
  37.7 38.2 %copy-start.3 = (f32[31,1536]{1,0:T(8,128)S(1)}, f32[31,1536]{1,0:T(8,128)}, u32[]{:S(2)}) copy-start(f32[31,1536]{1,0:T(8,128)} %param.14) | copy-start | bytes 571396
  60.2 15.9 %collective-permute-start.2 = (bf16[384,768]{1,0:T(8,128)(2,1)S(1)}, bf16[384,768]{1,0:T(8,128)(2,1)S(1)}, u32[]{:S(2)}, u32[]{:S(2)}) collective-permute-start(bf16[384,768]{1,0:T(8,128)(2,1)S(1)} %bitcast.30), channel_id=1, source_target_pairs={{0,1},{1,0},{2,3},{3,2},{4,5},{5,4},{6,7},{7,6},{8,9},{9,8},{10,11... | collective-permute-start | bytes 1769480 | tf_op jit(solution)/shard_map/ppermute | solution.py:423
  64.7 27.6 %collective-permute-start.3 = (bf16[384,768]{1,0:T(8,128)(2,1)S(1)}, bf16[384,768]{1,0:T(8,128)(2,1)S(1)}, u32[]{:S(2)}, u32[]{:S(2)}) collective-permute-start(bf16[384,768]{1,0:T(8,128)(2,1)S(1)} %bitcast.31), channel_id=1, source_target_pairs={{0,8},{8,16},{16,24},{24,0},{1,9},{9,17},{17,25},{25,1},{2,10},{10... | collective-permute-start | bytes 1769480 | tf_op jit(solution)/shard_map/ppermute | solution.py:417
  67.9 28.5 %collective-permute-start.4 = (bf16[384,768]{1,0:T(8,128)(2,1)S(1)}, bf16[384,768]{1,0:T(8,128)(2,1)S(1)}, u32[]{:S(2)}, u32[]{:S(2)}) collective-permute-start(bf16[384,768]{1,0:T(8,128)(2,1)S(1)} %bitcast.32), channel_id=1, source_target_pairs={{0,16},{8,24},{16,0},{24,8},{1,17},{9,25},{17,1},{25,9},{2,18},{10... | collective-permute-start | bytes 1769480 | tf_op jit(solution)/shard_map/ppermute | solution.py:417
  72.2 25.5 %collective-permute-start.5 = (bf16[384,768]{1,0:T(8,128)(2,1)S(1)}, bf16[384,768]{1,0:T(8,128)(2,1)}, u32[]{:S(2)}, u32[]{:S(2)}) collective-permute-start(bf16[384,768]{1,0:T(8,128)(2,1)S(1)} %bitcast.33), channel_id=1, source_target_pairs={{0,24},{8,0},{16,8},{24,16},{1,25},{9,1},{17,9},{25,17},{2,26},{10... | collective-permute-start | bytes 1769480 | tf_op jit(solution)/shard_map/ppermute | solution.py:417
  76.2 35.3 %copy-start = (bf16[1,192,1536]{2,1,0:T(8,128)(2,1)S(1)}, bf16[1,192,1536]{2,1,0:T(8,128)(2,1)}, u32[]{:S(2)}) copy-start(bf16[1,192,1536]{2,1,0:T(8,128)(2,1)} %param.15) | copy-start | bytes 1769476
  91.5 0.9 copy-start.2
  97.8 27.7 %all-to-all-start.1 = ((bf16[16,192,128]{2,1,0:T(8,128)(2,1)}), bf16[16,192,128]{2,1,0:T(8,128)(2,1)}, u32[]{:S(2)}, u32[]{:S(2)}) async-start(bf16[16,192,128]{2,1,0:T(8,128)(2,1)} %copy-done.2), calls=%async_computation.1 | async-start | bytes 1572864 | tf_op jit(solution)/shard_map/all_to_all | solution.py:436
  103.8 21.7 %collective-permute-start.8 = (bf16[384,768]{1,0:T(8,128)(2,1)S(1)}, bf16[384,768]{1,0:T(8,128)(2,1)}, u32[]{:S(2)}, u32[]{:S(2)}) collective-permute-start(bf16[384,768]{1,0:T(8,128)(2,1)S(1)} %collective-permute-done.3.refs_1_), channel_id=1, source_target_pairs={{0,1},{1,0},{2,3},{3,2},{4,5},{5,4},{6,7},{7,6},{8,9},{9,8},{10,11... | collective-permute-start | bytes 1769480 | tf_op jit(solution)/shard_map/ppermute | solution.py:428
  107.1 18.4 %collective-permute-start.9 = (bf16[384,768]{1,0:T(8,128)(2,1)S(1)}, bf16[384,768]{1,0:T(8,128)(2,1)}, u32[]{:S(2)}, u32[]{:S(2)}) collective-permute-start(bf16[384,768]{1,0:T(8,128)(2,1)S(1)} %collective-permute-done.4.refs_2_), channel_id=1, source_target_pairs={{0,1},{1,0},{2,3},{3,2},{4,5},{5,4},{6,7},{7,6},{8,9},{9,8},{10,11... | collective-permute-start | bytes 1769480 | tf_op jit(solution)/shard_map/ppermute | solution.py:428
  109.0 16.5 %collective-permute-start.10 = (bf16[384,768]{1,0:T(8,128)(2,1)}, bf16[384,768]{1,0:T(8,128)(2,1)}, u32[]{:S(2)}, u32[]{:S(2)}) collective-permute-start(bf16[384,768]{1,0:T(8,128)(2,1)} %collective-permute-done.5.refs_3_), channel_id=1, source_target_pairs={{0,1},{1,0},{2,3},{3,2},{4,5},{5,4},{6,7},{7,6},{8,9},{9,8},{10,11... | collective-permute-start | bytes 1769480 | tf_op jit(solution)/shard_map/ppermute | solution.py:428
  113.1 7.4 %collective-permute-start.6 = (bf16[48,1536]{1,0:T(8,128)(2,1)}, bf16[48,1536]{1,0:T(8,128)(2,1)S(1)}, u32[]{:S(2)}, u32[]{:S(2)}) collective-permute-start(bf16[48,1536]{1,0:T(8,128)(2,1)} %pad_maximum_fusion.1), channel_id=1, source_target_pairs={{0,32},{32,64},{64,96},{96,128},{128,160},{160,192},{192,224},{224... | collective-permute-start | bytes 442376 | tf_op jit(solution)/shard_map/ppermute | solution.py:432
  117.3 8.2 %collective-permute-start.7 = (bf16[48,1536]{1,0:T(8,128)(2,1)}, bf16[48,1536]{1,0:T(8,128)(2,1)}, u32[]{:S(2)}, u32[]{:S(2)}) collective-permute-start(bf16[48,1536]{1,0:T(8,128)(2,1)} %pad_maximum_fusion.2), channel_id=1, source_target_pairs={{32,0},{64,32},{96,64},{128,96},{160,128},{192,160},{224,192},{256... | collective-permute-start | bytes 442376 | tf_op jit(solution)/shard_map/ppermute | solution.py:434
  125.5 1.1 copy-start.1
  161.8 27.4 %all-to-all-start.3 = ((f32[16,16,128]{2,1,0:T(8,128)}), f32[16,16,128]{2,1,0:T(8,128)S(1)}, u32[]{:S(2)}, u32[]{:S(2)}) async-start(f32[16,16,128]{2,1,0:T(8,128)} %broadcast_in_dim.10), calls=%async_computation.3 | async-start | bytes 262144 | tf_op jit(solution)/shard_map/all_to_all | solution.py:392
